TPU v7x, 32 devices: a whole 2x2x4 slice. The times are simulated.
32 devices in a mesh: grp: 4 (over z), dp: 2 (over y), mp: 4 (over x, core).
Axes of the slice: x: 2, y: 2, z: 4, core: 2. Of those that a mesh axis runs over, the one named last changes fastest.
Arguments:
- tower_features: bfloat16 [4, 1024, 4096], P('grp', 'dp', 'mp'), may hold values from -6 to 6
- doc_weight: bfloat16 [4096, 1024], P('mp'), may hold values from -6 to 6
- query_weight: bfloat16 [4096, 1024], P('mp'), may hold values from -6 to 6
- positive_ids: int32 [1024], replicated, may hold values from 0 to 3071
Outputs:
- loss: float32 [], replicated
- doc_grad: float32 [4096, 1024], P('mp')
- query_grad: float32 [4096, 1024], P('mp')
- feature_grad: bfloat16 [4, 1024, 4096], P('grp', 'dp', 'mp')
All inputs are finite; a program needn't handle non-finite values.
Results may differ from a plain program's by a relative error of at most 0.003.
The roundings to bfloat16 on the way count: a program that leaves them out, or rounds other values in their place, can miss the bound.
Values may be sent and summed in bfloat16 or wider, within the bound.
A program may use at most 64 MiB of HBM per device.

v0:
```python
import jax
import jax.numpy as jnp
from jax import lax
from jax.sharding import PartitionSpec as P

inverse_temp = 200.0
epsilon_norm = 1e-06


def spread(value, axis, source):
    kept = jnp.where(lax.axis_index(axis) == source, value, 0).astype(value.dtype)
    return lax.psum(kept, axis)


def local(tower_features, doc_weight, query_weight, positive_ids):
    group_index = lax.axis_index("grp")
    is_query = group_index == 3
    passage_live = jnp.logical_not(is_query)
    features_local = tower_features[0]
    weight_local = jnp.where(is_query, query_weight, doc_weight)
    n_model = lax.axis_size("mp")
    per_device = features_local.shape[0] // n_model
    rows_in = features_local
    summed = lax.psum_scatter(
        jnp.dot(rows_in, weight_local, preferred_element_type=jnp.float32),
        "mp",
        scatter_dimension=0,
        tiled=True,
    )
    row_norms = jnp.sqrt(jnp.sum(summed * summed, axis=-1, keepdims=True) + epsilon_norm)
    unit_rows = summed / row_norms
    embedded = unit_rows.astype(jnp.bfloat16)
    query_piece = spread(embedded, "grp", 3)
    queries_all = lax.all_gather(query_piece, ("dp", "mp"), axis=0, tiled=True)
    total_q = queries_all.shape[0]
    logits_raw = inverse_temp * lax.dot_general(
        queries_all, embedded, (((1,), (1,)), ((), ())), preferred_element_type=jnp.float32
    )
    base_index = (
        group_index * total_q + (lax.axis_index("dp") * n_model + lax.axis_index("mp")) * per_device
    )
    column_ids = base_index + lax.broadcasted_iota(jnp.int32, (1, per_device), 1)
    positive_hit = jnp.logical_and(positive_ids[:, None] == column_ids, passage_live)
    logits = jnp.where(passage_live, logits_raw, -1e30)
    positive_part = jnp.sum(jnp.where(positive_hit, logits_raw, 0.0), axis=1)
    local_top = jnp.max(logits, axis=1)
    row_top = lax.pmax(local_top, ("grp", "dp", "mp"))
    local_total = jnp.sum(jnp.where(passage_live, jnp.exp(logits - row_top[:, None]), 0.0), axis=1)
    row_total, positive = lax.psum((local_total, positive_part), ("grp", "dp", "mp"))
    lse = row_top + jnp.log(row_total)
    loss = jnp.mean(lse - positive)
    probs = jnp.where(passage_live, jnp.exp(logits - lse[:, None]), 0.0)
    dlogit = ((probs - positive_hit.astype(jnp.float32)) / total_q).astype(jnp.bfloat16)
    in_group = lax.psum_scatter(
        inverse_temp * jnp.dot(dlogit, embedded, preferred_element_type=jnp.float32),
        ("dp", "mp"),
        scatter_dimension=0,
        tiled=True,
    )
    dquery = lax.psum(in_group, "grp")
    dpassage = inverse_temp * lax.dot_general(
        dlogit, queries_all, (((0,), (0,)), ((), ())), preferred_element_type=jnp.float32
    )
    grad_emb = jnp.where(is_query, dquery, dpassage)
    inner = jnp.sum(unit_rows * grad_emb, axis=-1, keepdims=True)
    grad_proj = ((grad_emb - unit_rows * inner) / row_norms).astype(jnp.bfloat16)
    gathered_rows = lax.all_gather(grad_proj, "mp", axis=0, tiled=True)
    rows_in = features_local
    weight_part = lax.dot_general(
        rows_in, gathered_rows, (((0,), (0,)), ((), ())), preferred_element_type=jnp.float32
    )
    back_rows = lax.dot_general(
        gathered_rows, weight_local, (((1,), (1,)), ((), ())), preferred_element_type=jnp.float32
    ).astype(jnp.bfloat16)
    feature_part = back_rows
    weight_part, feature_part = (weight_part, feature_part)
    doc_part = jnp.where(is_query, 0.0, weight_part)
    query_part = jnp.where(is_query, weight_part, 0.0)
    doc_grad, query_grad = lax.psum((doc_part, query_part), ("grp", "dp"))
    return (loss, doc_grad, query_grad, feature_part[None])


def solution(mesh):
    in_specs = (P("grp", "dp", "mp"), P("mp", None), P("mp", None), P())
    out_specs = (P(), P("mp", None), P("mp", None), P("grp", "dp", "mp"))
    return jax.shard_map(local, mesh=mesh, in_specs=in_specs, out_specs=out_specs, check_vma=False)
```

profile of v0, /device:TPU:0, one launch (start us, length us, event | category | flops | bytes accessed | tf_op | source)
XLA Modules:
  0.0 609.8 jit_solution(7120527639464607473)
XLA Ops:
  7.2 0.0 reduce-scatter.3.cloned.1.call-start
  7.2 1.2 copy-done
  8.4 4.2 convolution_bitcast_fusion
  12.6 0.0 reduce-scatter.3.cloned.1.call-update
  12.7 0.0 all-reduce.6.cloned.1.call-start
  12.7 34.2 %reduce-scatter.3.cloned.1.call-done = f32[128,1024]{0,1:T(8,128)} async-done(((f32[512,1024]{0,1:T(8,128)}), f32[128,1024]{0,1:T(8,128)}) %reduce-scatter.3.cloned.1.call-update) | async-done | bytes 524304 | tf_op jit(solution)/shard_map/reduce_scatter | solution.py:24
  46.9 1.2 multiply_reduce_fusion.1
  48.1 1.8 broadcast_select_fusion.3
  50.0 0.0 all-gather.3.cloned.1.call-start
  50.0 35.4 %all-reduce.6.cloned.1.call-done = bf16[128,1024]{0,1:T(8,128)(2,1)} async-done(((bf16[128,1024]{0,1:T(8,128)(2,1)}), bf16[128,1024]{0,1:T(8,128)(2,1)}) %all-reduce.6.cloned.1.call-update) | async-done | bytes 262160 | tf_op jit(solution)/shard_map/psum | solution.py:12
  85.5 0.0 reduce-scatter.5.cloned.1.call-start
  85.6 29.7 %all-gather.3.cloned.1.call-done = bf16[1024,1024]{0,1:T(8,128)(2,1)} async-done(((bf16[128,1024]{0,1:T(8,128)(2,1)}), bf16[1024,1024]{0,1:T(8,128)(2,1)}) %all-gather.3.cloned.1.call-update) | async-done | bytes 2097168 | tf_op jit(solution)/shard_map/all_gather | solution.py:34
  115.3 2.2 select_reduce_fusion.2
  117.5 39.4 %pmax.7 = f32[1024]{0:T(1024)S(1)} all-reduce(f32[1024]{0:T(1024)S(1)} %get-tuple-element.18), channel_id=1, replica_groups=mesh['grp'=4,'dp'=2,'mp'=4] {'grp','dp','mp'}, use_global_device_ids=true, to_apply=%region_4.5 | all-reduce | flops 1024 | bytes 8192 | tf_op jit(solution)/shard_map/pmax | solution.py:47
  156.9 0.2 select_reduce_fusion
  157.1 41.1 %all-reduce = (f32[1024]{0:T(1024)S(1)}, f32[1024]{0:T(1024)S(1)}) all-reduce(f32[1024]{0:T(1024)S(1)} %get-tuple-element.9, f32[1024]{0:T(1024)S(1)} %get-tuple-element.8), channel_id=1, replica_groups=mesh['grp'=4,'dp'=2,'mp'=4] {'grp','dp','mp'}, use_global_device_ids=true, to_apply=%region_6.7 | all-reduce | flops 2048 | bytes 16384 | tf_op jit(solution)/shard_map/psum | solution.py:49
  198.2 0.6 subtract_reduce_fusion
  198.8 2.9 convolution_multiply_fusion
  201.7 0.0 all-reduce.8.cloned.1.call-start
  201.8 51.2 %reduce-scatter.5.cloned.1.call-done = f32[128,1024]{0,1:T(8,128)} async-done(((f32[1024,1024]{0,1:T(8,128)}), f32[128,1024]{0,1:T(8,128)}) %reduce-scatter.5.cloned.1.call-update) | async-done | bytes 524304 | tf_op jit(solution)/shard_map/reduce_scatter | solution.py:54
  253.0 0.0 all-gather.5.cloned.1.call-start
  253.1 40.6 %all-reduce.8.cloned.1.call-done = f32[128,1024]{0,1:T(8,128)} async-done(((f32[128,1024]{0,1:T(8,128)}), f32[128,1024]{0,1:T(8,128)}) %all-reduce.8.cloned.1.call-update) | async-done | bytes 524304 | tf_op jit(solution)/shard_map/psum | solution.py:60
  293.6 2.5 multiply_reduce_fusion
  296.1 0.8 divide_convert_fusion
  296.9 0.0 all-reduce.10.cloned.1.call-start
  297.0 17.0 %all-gather.5.cloned.1.call-done = bf16[512,1024]{0,1:T(8,128)(2,1)} async-done(((bf16[128,1024]{0,1:T(8,128)(2,1)}), bf16[512,1024]{0,1:T(8,128)(2,1)}) %all-gather.5.cloned.1.call-update) | async-done | bytes 1048592 | tf_op jit(solution)/shard_map/all_gather | solution.py:67
  314.0 5.9 select_bitcast_fusion
  320.6 0.5 copy-done.2
  321.1 3.9 fusion
  325.0 266.2 %all-reduce.10.cloned.1.call-done = (f32[1024,1024]{0,1:T(8,128)}, f32[1024,1024]{0,1:T(8,128)}) async-done(((f32[1024,1024]{0,1:T(8,128)}, f32[1024,1024]{0,1:T(8,128)}), (f32[1024,1024]{0,1:T(8,128)}, f32[1024,1024]{0,1:T(8,128)})) %all-reduce.10.cloned.1.call-update) | async-done | bytes 8388624 | tf_op jit(solution)/shard_map/psum | solution.py:79
  591.2 5.3 copy.10
  596.5 5.3 copy.11
  (14 shorter events, 0.1 us)
Async XLA Ops:
  7.2 1.2 copy-start
  7.2 39.8 %reduce-scatter.3.cloned.1.call-start = ((), (), s32[]{:S(2)}) async-start(), calls=%async_computation.2 | async-start | bytes 2621440 | tf_op jit(solution)/shard_map/reduce_scatter | solution.py:24
  12.7 72.8 %all-reduce.6.cloned.1.call-start = ((), (), s32[]{:S(2)}) async-start(), calls=%async_computation.3 | async-start | bytes 524288 | tf_op jit(solution)/shard_map/psum | solution.py:12
  50.0 65.3 %all-gather.3.cloned.1.call-start = ((), (), s32[]{:S(2)}) async-start(), calls=%async_computation.4 | async-start | bytes 2359296 | tf_op jit(solution)/shard_map/all_gather | solution.py:34
  85.5 167.5 %reduce-scatter.5.cloned.1.call-start = ((), (), s32[]{:S(2)}) async-start(), calls=%async_computation.5 | async-start | bytes 4718592 | tf_op jit(solution)/shard_map/reduce_scatter | solution.py:54
  85.6 71.3 %copy-start.3 = (s32[1024]{0:T(1024)S(1)}, s32[1024]{0:T(1024)}, u32[]{:S(2)}) copy-start(s32[1024]{0:T(1024)} %param.7) | copy-start | bytes 12292
  85.6 113.2 %copy-start.1 = (f32[128,1024]{0,1:T(8,128)S(1)}, f32[128,1024]{0,1:T(8,128)}, u32[]{:S(2)}) copy-start(f32[128,1024]{0,1:T(8,128)} %reduce-scatter.3.cloned.1.call-done) | copy-start | bytes 1572868
  201.7 91.9 %all-reduce.8.cloned.1.call-start = ((), (), s32[]{:S(2)}) async-start(), calls=%async_computation.6 | async-start | bytes 1048576 | tf_op jit(solution)/shard_map/psum | solution.py:60
  253.0 61.0 %all-gather.5.cloned.1.call-start = ((), (), s32[]{:S(2)}) async-start(), calls=%async_computation.7 | async-start | bytes 1310720 | tf_op jit(solution)/shard_map/all_gather | solution.py:67
  296.9 294.2 %all-reduce.10.cloned.1.call-start = ((), (), s32[]{:S(2)}) async-start(), calls=%async_computation.8 | async-start | bytes 16777216 | tf_op jit(solution)/shard_map/psum | solution.py:79
  319.9 1.2 copy-start.2
Sparse Core Ops, SparseCore 0:
  12.8 34.1 reduce-scatter.2
  50.1 35.3 all-reduce.5
  87.4 27.9 all-gather.2
  201.9 51.1 reduce-scatter.4
  255.3 38.2 all-reduce.7
  297.1 16.8 all-gather.4
  320.0 271.0 all-reduce.9
where the time goes:
time: 610 us
  waiting for transfers between devices  474 us (78%)
  blocking collectives  80.5 us (13%)
  matrix products  21.5 us (4%)
  between operations  16.1 us (3%)
  local copies, waits for them, and re-layouts  12.3 us (2%)
    psum x1, waiting for transfers between devices, local(): doc_grad, query_grad = lax.psum((doc_part, query_part), ('grp', 'dp'))  266 us
    reduce_scatter x1, waiting for transfers between devices, local(): lax.psum_scatter(inverse_temp * jnp.dot(dlogit, embedded, preferred_eleme...  51.2 us
    psum x1, blocking collectives, local(): lax.psum((local_total, positive_part), ('grp', 'dp', 'mp'))  41.1 us
    psum x1, waiting for transfers between devices, local(): dquery = lax.psum(in_group, 'grp')  40.6 us
    pmax x1, blocking collectives, local(): row_top = lax.pmax(local_top, ('grp', 'dp', 'mp'))  39.4 us
    psum x1, waiting for transfers between devices, spread(): return lax.psum(kept, axis)  35.4 us
    reduce_scatter x1, waiting for transfers between devices, local(): lax.psum_scatter(jnp.dot(rows_in, weight_local, preferred_element_type=jn...  34.2 us
    all_gather x1, waiting for transfers between devices, local(): queries_all = lax.all_gather(query_piece, ('dp', 'mp'), axis=0, tiled=True)  29.7 us
  transfers between devices with their start and end apart: 7, of which 7 were waited for; matrix products, arithmetic and copies ran while one was open for 1% of the time, Pallas kernels for 0%

commit v1 on v0

v1 whole, which is shorter than its diff:
```python
import functools

import jax
import jax.numpy as jnp
from jax import lax
from jax.experimental import pallas as pl
from jax.experimental.pallas import tpu as pltpu
from jax.sharding import PartitionSpec as P

inverse_temp = 200.0
epsilon_norm = 1e-06
MESH = pl.DeviceIdType.MESH
VMEM = pl.BlockSpec(memory_space=pltpu.VMEM)
LIMIT = 50 * 1024 * 1024


def place():
    mp = lax.axis_index("mp")
    return lax.axis_index("grp"), lax.axis_index("dp"), mp // 2, lax.rem(mp, 2)


def meet(targets):
    barrier = pltpu.get_barrier_semaphore()
    for target in targets:
        pl.semaphore_signal(barrier, inc=1, device_id=target, device_id_type=MESH)
    pl.semaphore_wait(barrier, len(targets))


def remote(src, dst, send, recv, target):
    return pltpu.make_async_remote_copy(
        src_ref=src, dst_ref=dst, send_sem=send, recv_sem=recv, device_id=target, device_id_type=MESH
    )


def params(collective):
    return pltpu.CompilerParams(
        collective_id=collective, has_side_effects=True, vmem_limit_bytes=LIMIT
    )


def gather_kernel(n_grp, n_dp, n_chip, chunks, spread, x_ref, out_ref, zs, zr, ls, lr, fs, fr):
    grp, dp, chip, core = place()
    rows = x_ref.shape[0] // chunks
    offsets = [(d, k) for d in range(n_dp) for k in range(n_chip) if d or k]

    def slot(d, k):
        return (lax.rem(dp + n_dp + d, n_dp) * n_chip + lax.rem(chip + n_chip + k, n_chip)) * 2 + core

    def peer(d, k):
        to = {"mp": lax.rem(chip + k, n_chip) * 2 + core}
        if n_dp > 1:
            to["dp"] = lax.rem(dp + d, n_dp)
        return to

    sibling = {"mp": chip * 2 + 1 - core}
    targets = [sibling] + [peer(d, k) for d, k in offsets]
    if spread:
        targets += [{"grp": lax.rem(grp + 1, n_grp)}, {"grp": lax.rem(grp + n_grp - 1, n_grp)}]
    meet(targets)
    own = slot(0, 0)
    last = grp == n_grp - 1
    below = {"grp": lax.rem(grp + n_grp - 1, n_grp)}

    def part(c, index):
        return out_ref.at[index, pl.ds(c * rows, rows)]

    def hop(c):
        return remote(part(c, own), part(c, own), zs.at[c], zr.at[c], below)

    if spread:

        @pl.when(last)
        def _():
            out_ref[own] = x_ref[...]

    else:
        out_ref[own] = x_ref[...]
    sent = []
    for c in range(chunks):
        if spread:

            @pl.when(jnp.logical_not(last))
            def _():
                hop(c).wait_recv()

            @pl.when(grp > 0)
            def _():
                hop(c).start()

        for i, (d, k) in enumerate(offsets):
            copy = remote(part(c, own), part(c, own), ls.at[c, i], lr.at[c, i], peer(d, k))
            copy.start()
            sent.append(copy)
        copy = remote(part(c, own), part(c, own), fs.at[c, len(offsets)], fr.at[c, len(offsets)], sibling)
        copy.start()
        sent.append(copy)
    forwarded = []
    for c in range(chunks):
        for i, (d, k) in enumerate(offsets):
            remote(part(c, own), part(c, own), ls.at[c, i], lr.at[c, i], peer(d, k)).wait_recv()
            came = slot(-d, -k)
            copy = remote(part(c, came), part(c, came), fs.at[c, i], fr.at[c, i], sibling)
            copy.start()
            forwarded.append(copy)
    for copy in forwarded:
        copy.wait()
    for c in range(chunks):
        for i in range(len(offsets)):
            sent[c * (len(offsets) + 1) + i].wait_send()
        sent[c * (len(offsets) + 1) + len(offsets)].wait()
        if spread:

            @pl.when(grp > 0)
            def _():
                hop(c).wait_send()


def gather(x, n_grp, n_dp, n_chip, chunks, spread, collective):
    peers = max(n_dp * n_chip - 1, 1)
    dma = pltpu.SemaphoreType.DMA
    return pl.pallas_call(
        functools.partial(gather_kernel, n_grp, n_dp, n_chip, chunks, spread),
        out_shape=jax.ShapeDtypeStruct((n_dp * n_chip * 2,) + x.shape, x.dtype),
        in_specs=[VMEM],
        out_specs=VMEM,
        scratch_shapes=[
            dma((chunks,)), dma((chunks,)),
            dma((chunks, peers)), dma((chunks, peers)),
            dma((chunks, peers + 1)), dma((chunks, peers + 1)),
        ],
        compiler_params=params(collective),
    )(x)


def scatter_kernel(n_grp, n_dp, n_chip, down, steps, x_ref, out_ref, near, far_out, far, zbuf, ns, nr, fs, fr, zs, zr):
    grp, dp, chip, core = place()
    offsets = [(d, k) for d in range(n_dp) for k in range(n_chip)]
    offsets = offsets[1:] + offsets[:1]
    sibling = {"mp": chip * 2 + 1 - core}

    def slot(d, k, c):
        return (lax.rem(dp + d, n_dp) * n_chip + lax.rem(chip + k, n_chip)) * 2 + c

    def peer(d, k):
        to = {"mp": lax.rem(chip + k, n_chip) * 2 + core}
        if n_dp > 1:
            to["dp"] = lax.rem(dp + d, n_dp)
        return to

    targets = [sibling] + [peer(d, k) for d, k in offsets[:-1]]
    if down:
        targets += [{"grp": lax.rem(grp + 1, n_grp)}, {"grp": lax.rem(grp + n_grp - 1, n_grp)}]
    meet(targets)
    first = []
    for i, (d, k) in enumerate(offsets):
        copy = remote(x_ref.at[slot(d, k, 1 - core)], near.at[i], ns.at[i], nr.at[i], sibling)
        copy.start()
        first.append(copy)
    second = []
    for i, (d, k) in enumerate(offsets[:-1]):
        first[i].wait_recv()
        far_out[i] = (x_ref[slot(d, k, core)] + near[i]).astype(far_out.dtype)
        copy = remote(far_out.at[i], far.at[i], fs.at[i], fr.at[i], peer(d, k))
        copy.start()
        second.append(copy)
    first[-1].wait_recv()
    total = x_ref[slot(0, 0, core)] + near[len(offsets) - 1]
    for i, copy in enumerate(second):
        copy.wait_recv()
        total = total + far[i].astype(jnp.float32)
    out_ref[...] = total
    for copy in first + second:
        copy.wait_send()
    if down:
        last = n_grp - 1
        rows = out_ref.shape[0] // steps
        after = {"grp": lax.rem(grp + 1, n_grp)}

        def hop(c):
            piece = pl.ds(c * rows, rows)
            return remote(out_ref.at[piece], zbuf.at[piece], zs.at[c], zr.at[c], after)

        for c in range(steps):

            @pl.when(grp > 0)
            def _():
                hop(c).wait_recv()
                piece = pl.ds(c * rows, rows)
                out_ref[piece] = out_ref[piece] + zbuf[piece]

            @pl.when(grp < last)
            def _():
                hop(c).start()

        for c in range(steps):

            @pl.when(grp < last)
            def _():
                hop(c).wait_send()


def scatter(x, n_grp, n_dp, n_chip, wire, down, collective):
    count = n_dp * n_chip
    block = x.shape[1:]
    dma = pltpu.SemaphoreType.DMA
    z_block = block if down else (16, 128)
    peers = max(count - 1, 1)
    return pl.pallas_call(
        functools.partial(scatter_kernel, n_grp, n_dp, n_chip, down, 8),
        out_shape=jax.ShapeDtypeStruct(block, jnp.float32),
        in_specs=[VMEM],
        out_specs=VMEM,
        scratch_shapes=[
            pltpu.VMEM((count,) + block, jnp.float32),
            pltpu.VMEM((peers,) + block, wire),
            pltpu.VMEM((peers,) + block, wire),
            pltpu.VMEM(z_block, jnp.float32),
            dma((count,)), dma((count,)),
            dma((peers,)), dma((peers,)),
            dma((8,)), dma((8,)),
        ],
        compiler_params=params(collective),
    )(x)


def stats_kernel(n_grp, n_dp, n_mp, x_ref, out_ref, layer, mid, other, ls, lr, zs, zr):
    grp, dp = lax.axis_index("grp"), lax.axis_index("dp")
    mp = lax.axis_index("mp")
    offsets = [(d, m) for d in range(n_dp) for m in range(n_mp) if d or m]

    def peer(d, m):
        return {"dp": lax.rem(dp + d, n_dp), "mp": lax.rem(mp + m, n_mp)}

    ups = [{"grp": lax.rem(grp + i, n_grp)} for i in range(1, n_grp)]
    meet([peer(d, m) for d, m in offsets] + ups)
    copies = []
    for i, (d, m) in enumerate(offsets):
        copy = remote(x_ref, layer.at[i], ls.at[i], lr.at[i], peer(d, m))
        copy.start()
        copies.append(copy)
    for copy in copies:
        copy.wait()

    def merge(parts):
        top = parts[0][0]
        for part in parts[1:]:
            top = jnp.maximum(top, part[0])
        total = parts[0][1] * jnp.exp(parts[0][0] - top)
        positive = parts[0][2]
        for part in parts[1:]:
            total = total + part[1] * jnp.exp(part[0] - top)
            positive = positive + part[2]
        return top, total, positive

    got = merge([tuple(x_ref[j] for j in range(3))] + [tuple(layer[i, j] for j in range(3)) for i in range(len(offsets))])
    for j in range(3):
        mid[j] = got[j]
    copies = []
    for i, up in enumerate(ups):
        copy = remote(mid, other.at[i], zs.at[i], zr.at[i], up)
        copy.start()
        copies.append(copy)
    for copy in copies:
        copy.wait()
    got = merge([got] + [tuple(other[i, j] for j in range(3)) for i in range(len(ups))])
    for j in range(3):
        out_ref[j] = got[j]


def stats(x, n_grp, n_dp, n_mp, collective):
    dma = pltpu.SemaphoreType.DMA
    peers = n_dp * n_mp - 1
    return pl.pallas_call(
        functools.partial(stats_kernel, n_grp, n_dp, n_mp),
        out_shape=jax.ShapeDtypeStruct(x.shape, x.dtype),
        in_specs=[VMEM],
        out_specs=VMEM,
        scratch_shapes=[
            pltpu.VMEM((peers,) + x.shape, x.dtype),
            pltpu.VMEM(x.shape, x.dtype),
            pltpu.VMEM((n_grp - 1,) + x.shape, x.dtype),
            dma((peers,)), dma((peers,)),
            dma((n_grp - 1,)), dma((n_grp - 1,)),
        ],
        compiler_params=params(collective),
    )(x)


def grads_kernel(n_grp, n_dp, chunks, x_ref, doc, query, mine, parts, ps, pr, ds, dr, qs, qr, yds, ydr, yqs, yqr):
    grp, dp = lax.axis_index("grp"), lax.axis_index("dp")
    last = n_grp - 1
    root = 1
    rows = x_ref.shape[0] // chunks
    up = {"grp": lax.rem(grp + 1, n_grp)}
    under = {"grp": lax.rem(grp + n_grp - 1, n_grp)}
    aside = [{"dp": lax.rem(dp + d, n_dp)} for d in range(1, n_dp)]
    meet([{"grp": lax.rem(grp + i, n_grp)} for i in range(1, n_grp)] + aside)
    is_root = grp == root
    is_query = grp == last
    feeds = jnp.logical_and(jnp.logical_not(is_root), jnp.logical_not(is_query))
    others = [g for g in range(last) if g != root]
    index = jnp.where(grp > root, grp - 1, 0)

    def piece(c):
        return pl.ds(c * rows, rows)

    def feed(c, i):
        return remote(mine.at[piece(c)], parts.at[i, piece(c)], ps.at[c], pr.at[c, i], {"grp": root})

    def doc_hop(c, to, i):
        here = doc.at[dp, piece(c)]
        return remote(here, here, ds.at[c, i], dr.at[c], to)

    def query_hop(c):
        here = query.at[dp, piece(c)]
        return remote(here, here, qs.at[c], qr.at[c], under)

    def doc_side(c, i):
        here = doc.at[dp, piece(c)]
        return remote(here, here, yds.at[c, i], ydr.at[c, i], aside[i])

    def query_side(c, i):
        here = query.at[dp, piece(c)]
        return remote(here, here, yqs.at[c, i], yqr.at[c, i], aside[i])

    for c in range(chunks):

        @pl.when(feeds)
        def _():
            mine[piece(c)] = x_ref[piece(c)].astype(jnp.bfloat16)
            feed(c, index).start()

        @pl.when(is_query)
        def _():
            query[dp, piece(c)] = x_ref[piece(c)].astype(jnp.bfloat16)
            query_hop(c).start()
            for i in range(n_dp - 1):
                query_side(c, i).start()

    for c in range(chunks):

        @pl.when(is_root)
        def _():
            total = x_ref[piece(c)]
            for i in range(len(others)):
                feed(c, i).wait_recv()
                total = total + parts[i, piece(c)].astype(jnp.float32)
            doc[dp, piece(c)] = total.astype(jnp.bfloat16)
            doc_hop(c, under, 0).start()
            doc_hop(c, up, 1).start()

        @pl.when(jnp.logical_not(is_root))
        def _():
            doc_hop(c, up, 0).wait_recv()

        @pl.when(jnp.logical_and(grp > root, grp < last))
        def _():
            doc_hop(c, up, 0).start()

        for i in range(n_dp - 1):
            doc_side(c, i).start()

        @pl.when(jnp.logical_not(is_query))
        def _():
            query_hop(c).wait_recv()
            for i in range(n_dp - 1):
                query_side(c, i).start()

        @pl.when(jnp.logical_and(grp > 0, grp < last))
        def _():
            query_hop(c).start()

    for c in range(chunks):

        @pl.when(feeds)
        def _():
            feed(c, index).wait_send()

        @pl.when(is_root)
        def _():
            doc_hop(c, under, 0).wait_send()
            doc_hop(c, up, 1).wait_send()

        @pl.when(jnp.logical_and(grp > root, grp < last))
        def _():
            doc_hop(c, up, 0).wait_send()

        @pl.when(grp > 0)
        def _():
            query_hop(c).wait_send()

        for i in range(n_dp - 1):
            doc_side(c, i).wait()
            query_side(c, i).wait()


def grads(x, n_grp, n_dp, chunks, collective):
    dma = pltpu.SemaphoreType.DMA
    shape = jax.ShapeDtypeStruct((n_dp,) + x.shape, jnp.bfloat16)
    side = max(n_dp - 1, 1)
    return pl.pallas_call(
        functools.partial(grads_kernel, n_grp, n_dp, chunks),
        out_shape=(shape, shape),
        in_specs=[VMEM],
        out_specs=(VMEM, VMEM),
        scratch_shapes=[
            pltpu.VMEM(x.shape, jnp.bfloat16),
            pltpu.VMEM((n_grp - 2,) + x.shape, jnp.bfloat16),
            dma((chunks,)), dma((chunks, n_grp - 2)),
            dma((chunks, 2)), dma((chunks,)),
            dma((chunks,)), dma((chunks,)),
            dma((chunks, side)), dma((chunks, side)),
            dma((chunks, side)), dma((chunks, side)),
        ],
        compiler_params=params(collective),
    )(x)


def local(tower_features, doc_weight, query_weight, positive_ids):
    n_grp, n_dp, n_mp = (lax.axis_size(a) for a in ("grp", "dp", "mp"))
    n_chip = n_mp // 2
    grp, dp, mp = (lax.axis_index(a) for a in ("grp", "dp", "mp"))
    is_query = grp == n_grp - 1
    passage_live = jnp.logical_not(is_query)
    features = tower_features[0]
    rows, width = features.shape
    embed = doc_weight.shape[1]
    per_device = rows // n_mp
    half = width // n_dp
    blocks = [
        lax.dynamic_slice_in_dim(features, lax.rem(dp + s, n_dp) * half, half, axis=1)
        for s in range(n_dp)
    ]
    swapped = [
        lax.ppermute(blocks[s], "dp", [(i, (i + s) % n_dp) for i in range(n_dp)]) if s else blocks[0]
        for s in range(n_dp)
    ]
    weight = jnp.where(is_query, query_weight, doc_weight)
    projected = jnp.dot(features, weight, preferred_element_type=jnp.float32)
    summed = scatter(
        projected.reshape(n_mp, per_device, embed), n_grp, 1, n_chip, jnp.float32, False, 0
    )
    row_norms = jnp.sqrt(jnp.sum(summed * summed, axis=-1, keepdims=True) + epsilon_norm)
    unit_rows = summed / row_norms
    embedded = unit_rows.astype(jnp.bfloat16)
    queries_all = gather(embedded, n_grp, n_dp, n_chip, 4, True, 1).reshape(-1, embed)
    total_q = queries_all.shape[0]
    logits = inverse_temp * lax.dot_general(
        queries_all, embedded, (((1,), (1,)), ((), ())), preferred_element_type=jnp.float32
    )
    base_index = grp * total_q + (dp * n_mp + mp) * per_device
    column_ids = base_index + lax.broadcasted_iota(jnp.int32, (1, per_device), 1)
    positive_hit = jnp.logical_and(positive_ids[:, None] == column_ids, passage_live)
    positive_part = jnp.sum(jnp.where(positive_hit, logits, 0.0), axis=1)
    local_top = jnp.where(passage_live, jnp.max(logits, axis=1), -1e30)
    local_total = jnp.where(passage_live, jnp.sum(jnp.exp(logits - jnp.max(logits, axis=1, keepdims=True)), axis=1), 0.0)
    mine = jnp.stack([local_top, local_total, positive_part]).reshape(3, total_q // 128, 128)
    top, total, positive = stats(mine, n_grp, n_dp, n_mp, 2).reshape(3, total_q)
    lse = top + jnp.log(total)
    loss = jnp.mean(lse - positive)
    probs = jnp.where(passage_live, jnp.exp(jnp.where(passage_live, logits - lse[:, None], 0.0)), 0.0)
    dlogit = ((probs - positive_hit.astype(jnp.float32)) / total_q).astype(jnp.bfloat16)
    dq_part = inverse_temp * jnp.dot(dlogit, embedded, preferred_element_type=jnp.float32)
    dquery = scatter(
        dq_part.reshape(n_dp * n_mp, per_device, embed), n_grp, n_dp, n_chip, jnp.float32, True, 3
    )
    dpassage = inverse_temp * lax.dot_general(
        dlogit, queries_all, (((0,), (0,)), ((), ())), preferred_element_type=jnp.float32
    )
    grad_emb = jnp.where(is_query, dquery, dpassage)
    inner = jnp.sum(unit_rows * grad_emb, axis=-1, keepdims=True)
    grad_proj = ((grad_emb - unit_rows * inner) / row_norms).astype(jnp.bfloat16)
    dy = gather(grad_proj, n_grp, n_dp, n_chip, 1, False, 4).reshape(n_dp, rows, embed)
    grad_half = None
    for s in range(n_dp):
        term = lax.dot_general(
            swapped[s],
            lax.dynamic_index_in_dim(dy, lax.rem(dp + n_dp - s, n_dp), 0, keepdims=False),
            (((0,), (0,)), ((), ())),
            preferred_element_type=jnp.float32,
        )
        grad_half = term if grad_half is None else grad_half + term
    doc16, query16 = grads(grad_half, n_grp, n_dp, 8, 5)
    back = lax.dot_general(
        lax.dynamic_index_in_dim(dy, dp, 0, keepdims=False), weight, (((1,), (1,)), ((), ())),
        preferred_element_type=jnp.float32,
    ).astype(jnp.bfloat16)
    doc_grad = doc16.reshape(width, embed).astype(jnp.float32)
    query_grad = query16.reshape(width, embed).astype(jnp.float32)
    return (loss, doc_grad, query_grad, back[None])


def solution(mesh):
    in_specs = (P("grp", "dp", "mp"), P("mp", None), P("mp", None), P())
    out_specs = (P(), P("mp", None), P("mp", None), P("grp", "dp", "mp"))
    return jax.shard_map(local, mesh=mesh, in_specs=in_specs, out_specs=out_specs, check_vma=False)
```

time: 610 us -> 245 us (0.40)
  waiting for transfers between devices: 474 us -> 0.01 us
  Pallas kernels: 0 us -> 216 us
  blocking collectives: 80.5 us -> 0 us
  between operations: 16.1 us -> 2.59 us
  local copies, waits for them, and re-layouts: 12.3 us -> 3.52 us
  matrix products: 21.5 us -> 13.3 us
    psum x3 -> x0, waiting for transfers between devices: 342 us -> none  [the longest x1 266 us: local(): doc_grad, query_grad = lax.psum((doc_part, query_part), ('grp', 'dp'))]
    pallas_call x0 -> x6, Pallas kernels: none -> 216 us  [the longest x1 107 us: grads(): pl.pallas_call(functools.partial(grads_kernel, n_grp, n_dp, chunks), out_...]
    reduce_scatter x2 -> x0, waiting for transfers between devices: 85.5 us -> none  [the longest x1 51.2 us: local(): lax.psum_scatter(inverse_temp * jnp.dot(dlogit, embedded, preferred_eleme...]
    all_gather x2 -> x0, waiting for transfers between devices: 46.7 us -> none  [the longest x1 29.7 us: local(): queries_all = lax.all_gather(query_piece, ('dp', 'mp'), axis=0, tiled=True)]
    psum x1 -> x0, blocking collectives: 41.1 us -> none  [local(): lax.psum((local_total, positive_part), ('grp', 'dp', 'mp'))]
    pmax x1 -> x0, blocking collectives: 39.4 us -> none  [local(): row_top = lax.pmax(local_top, ('grp', 'dp', 'mp'))]
    unnamed x10, local copies, waits for them, and re-layouts: 12.3 us -> 2.69 us
    dot_general x3 -> x4, matrix products: 14 us -> 8.95 us  [the longest x2 3.83 us: local(): lax.dot_general(swapped[s], lax.dynamic_index_in_dim(dy, lax.rem(dp + n_d...]
  transfers between devices with their start and end apart: 7 -> 1, of which waited for: 7 -> 0; matrix products, arithmetic and copies ran while one was open for 1% -> 5% of each run, Pallas kernels for 0% -> 45%
where the time goes in v1:
time: 245 us
  Pallas kernels  216 us (88%)
  matrix products  13.3 us (5%)
  other arithmetic  6.46 us (3%)
  local copies, waits for them, and re-layouts  3.52 us (1%)
  starting transfers between devices  2.97 us (1%)
  between operations  2.59 us (1%)
    pallas_call x1, Pallas kernels, grads(): pl.pallas_call(functools.partial(grads_kernel, n_grp, n_dp, chunks), out_...  107 us
    pallas_call x2, Pallas kernels, scatter(): pl.pallas_call(functools.partial(scatter_kernel, n_grp, n_dp, n_chip, dow...  58.5 us
    pallas_call x2, Pallas kernels, gather(): pl.pallas_call(functools.partial(gather_kernel, n_grp, n_dp, n_chip, chun...  42.2 us
    pallas_call x1, Pallas kernels, stats(): pl.pallas_call(functools.partial(stats_kernel, n_grp, n_dp, n_mp), out_sh...  8.73 us
  transfers between devices with their start and end apart: 1, of which 0 were waited for; matrix products, arithmetic and copies ran while one was open for 5% of the time, Pallas kernels for 45%

profile of v1, /device:TPU:0, one launch (start us, length us, event | category | flops | bytes accessed | tf_op | source)
XLA Modules:
  0.0 244.9 jit_solution(3153096624448725185)
XLA Ops:
  0.6 0.0 copy-start
  0.7 1.2 copy-done
  1.9 0.8 dynamic-slice_bitcast_fusion
  2.7 3.0 %collective-permute-start = (bf16[512,512]{1,0:T(8,128)(2,1)}, bf16[512,512]{1,0:T(8,128)(2,1)}, u32[]{:S(2)}, u32[]{:S(2)}) collective-permute-start(bf16[512,512]{1,0:T(8,128)(2,1)} %dynamic-slice_bitcast_fusion), channel_id=1, source_target_pairs={{0,4},{4,0},{1,5},{5,1},{2,6},{6,2},{3,7},{7,3},{8,12},{12,8},{9,1... | collective-permute-start | bytes 1572872 | tf_op jit(solution)/shard_map/ppermute | solution.py:435
  5.7 2.9 %fusion.6 = f32[1024,512]{0,1:T(8,128)S(1)} fusion(bf16[1,512,1024]{2,1,0:T(8,128)(2,1)S(1)} %copy-done, bf16[1024,1024]{1,0:T(8,128)(2,1)} %param.6, bf16[1024,1024]{1,0:T(8,128)(2,1)} %param.5, pred[]{:T(512)S(6)} %eq.16), kind=kOutput, calls=%fused_computation.14 | convolution fusion | flops 1074790400 | bytes 7340033 | tf_op jit(solution)/shard_map/dot_general | solution.py:439
  8.5 16.3 %shard_map.75 = f32[128,1024]{1,0:T(8,128)S(1)} custom-call(f32[4,128,1024]{2,1,0:T(8,128)S(1)} %bitcast.48), custom_call_target="tpu_custom_call" | custom-call | tf_op jit(solution)/shard_map/pallas_call | solution.py:208
  24.9 0.1 multiply_reduce_fusion.1
  25.0 0.1 fusion.17.x_ref
  25.1 0.0 copy-start.2
  25.1 26.1 %shard_map.76 = bf16[8,128,1024]{2,1,0:T(8,128)(2,1)S(1)} custom-call(bf16[128,1024]{1,0:T(8,128)(2,1)S(1)} %fusion.17.x_ref), custom_call_target="tpu_custom_call" | custom-call | tf_op jit(solution)/shard_map/pallas_call | solution.py:121
  51.3 0.8 fusion.18
  52.1 0.0 copy-done.2
  52.1 0.2 exponential_reduce_fusion
  52.4 8.7 %shard_map.77 = f32[3,8,128]{2,1,0:T(8,128)S(1)} custom-call(f32[3,8,128]{2,1,0:T(8,128)S(1)} %pad_maximum_fusion.x_ref), custom_call_target="tpu_custom_call" | custom-call | tf_op jit(solution)/shard_map/pallas_call | solution.py:273
  61.1 0.6 fusion.16
  61.7 2.9 %convolution_multiply_fusion = f32[1024,1024]{1,0:T(8,128)} fusion(bf16[128,1024]{1,0:T(8,128)(2,1)S(1)} %fusion.17.x_ref, f32[1024,128]{0,1:T(8,128)S(1)} %get-tuple-element.13, f32[1024]{0:T(1024)S(1)} %get-tuple-element.10, s32[1024]{0:T(1024)S(1)} %copy-done.2, s32[128]{0:T(128)S(1)} %iota_add_fusion, pred[]{:T(512)S(6)} %not.3), kind=kOutput, calls=%fused_computation | convolution fusion | flops 270663680 | bytes 4989441 | tf_op jit(solution)/shard_map/dot_general | solution.py:463
  64.6 42.1 %shard_map.78 = f32[128,1024]{1,0:T(8,128)S(1)} custom-call(f32[8,128,1024]{2,1,0:T(8,128)} %bitcast.49), custom_call_target="tpu_custom_call" | custom-call | tf_op jit(solution)/shard_map/pallas_call | solution.py:208
  106.7 0.7 multiply_reduce_fusion
  107.4 0.2 divide_convert_fusion.x_ref
  107.6 16.0 %shard_map.79 = bf16[8,128,1024]{2,1,0:T(8,128)(2,1)S(1)} custom-call(bf16[128,1024]{1,0:T(8,128)(2,1)S(1)} %divide_convert_fusion.x_ref), custom_call_target="tpu_custom_call" | custom-call | tf_op jit(solution)/shard_map/pallas_call | solution.py:121
  124.3 0.0 copy-start.3
  124.3 0.0 copy-start.4
  124.3 0.7 fusion.4
  125.1 0.8 copy-done.3
  125.9 0.6 copy-done.4
  126.5 2.3 fusion
  128.8 0.0 collective-permute-done
  128.8 3.1 %convolution_add_fusion.x_ref = f32[512,1024]{1,0:T(8,128)} fusion(f32[512,1024]{1,0:T(8,128)S(1)} %fusion.4, bf16[512,512]{1,0:T(8,128)(2,1)} %collective-permute-done, bf16[2,512,1024]{2,1,0:T(8,128)(2,1)S(1)} %bitcast.47, s32[]{:T(128)S(6)} %select_n.95), kind=kOutput, calls=%fused_computation.4 | convolution fusion | flops 537395200 | bytes 5767172 | tf_op jit(solution)/shard_map/dot_general | solution.py:476
  131.9 106.6 %shard_map.80 = (bf16[2,512,1024]{2,1,0:T(8,128)(2,1)S(1)}, bf16[2,512,1024]{2,1,0:T(8,128)(2,1)}) custom-call(f32[512,1024]{1,0:T(8,128)} %convolution_add_fusion.x_ref), custom_call_target="tpu_custom_call" | custom-call | tf_op jit(solution)/shard_map/pallas_call | solution.py:401
  238.5 2.6 %bitcast_convert_fusion.1 = f32[1024,1024]{1,0:T(8,128)} fusion(bf16[2,512,1024]{2,1,0:T(8,128)(2,1)S(1)} %get-tuple-element.6), kind=kLoop, calls=%fused_computation.2 | loop fusion | flops 1048576 | bytes 6291456 | tf_op jit(solution)/shard_map/convert_element_type | solution.py:488
  241.1 0.0 copy-done.1
  241.1 2.6 %bitcast_convert_fusion = f32[1024,1024]{1,0:T(8,128)} fusion(bf16[2,512,1024]{2,1,0:T(8,128)(2,1)S(1)} %copy-done.1), kind=kLoop, calls=%fused_computation.1 | loop fusion | flops 1048576 | bytes 6291456 | tf_op jit(solution)/shard_map/convert_element_type | solution.py:489
  (5 shorter events, 0.0 us)
Async XLA Ops:
  0.6 1.2 copy-start
  2.7 126.1 %collective-permute-start = (bf16[512,512]{1,0:T(8,128)(2,1)}, bf16[512,512]{1,0:T(8,128)(2,1)}, u32[]{:S(2)}, u32[]{:S(2)}) collective-permute-start(bf16[512,512]{1,0:T(8,128)(2,1)} %dynamic-slice_bitcast_fusion), channel_id=1, source_target_pairs={{0,4},{4,0},{1,5},{5,1},{2,6},{6,2},{3,7},{7,3},{8,12},{12,8},{9,1... | collective-permute-start | bytes 1572872 | tf_op jit(solution)/shard_map/ppermute | solution.py:435
  25.1 27.0 %copy-start.2 = (s32[1024]{0:T(1024)S(1)}, s32[1024]{0:T(1024)}, u32[]{:S(2)}) copy-start(s32[1024]{0:T(1024)} %param.7) | copy-start | bytes 12292
  124.3 1.6 copy-start.3
  124.3 2.2 copy-start.4
  238.5 2.6 %copy-start.1 = (bf16[2,512,1024]{2,1,0:T(8,128)(2,1)S(1)}, bf16[2,512,1024]{2,1,0:T(8,128)(2,1)}, u32[]{:S(2)}) copy-start(bf16[2,512,1024]{2,1,0:T(8,128)(2,1)} %get-tuple-element.7) | copy-start | bytes 6291460

commit v2 on v1

--- a/solution.py
+++ b/solution.py
@@ -286,7 +286,7 @@
     )(x)
 
 
-def grads_kernel(n_grp, n_dp, chunks, x_ref, doc, query, mine, parts, ps, pr, ds, dr, qs, qr, yds, ydr, yqs, yqr):
+def grads_kernel(n_grp, n_dp, chunks, x_ref, doc, mine, parts, ps, pr, ds, dr, yds, ydr):
     grp, dp = lax.axis_index("grp"), lax.axis_index("dp")
     last = n_grp - 1
     root = 1
@@ -296,8 +296,7 @@
     aside = [{"dp": lax.rem(dp + d, n_dp)} for d in range(1, n_dp)]
     meet([{"grp": lax.rem(grp + i, n_grp)} for i in range(1, n_grp)] + aside)
     is_root = grp == root
-    is_query = grp == last
-    feeds = jnp.logical_and(jnp.logical_not(is_root), jnp.logical_not(is_query))
+    feeds = jnp.logical_and(jnp.logical_not(is_root), grp < last)
     others = [g for g in range(last) if g != root]
     index = jnp.where(grp > root, grp - 1, 0)
 
@@ -311,31 +310,16 @@
         here = doc.at[dp, piece(c)]
         return remote(here, here, ds.at[c, i], dr.at[c], to)
 
-    def query_hop(c):
-        here = query.at[dp, piece(c)]
-        return remote(here, here, qs.at[c], qr.at[c], under)
-
     def doc_side(c, i):
         here = doc.at[dp, piece(c)]
         return remote(here, here, yds.at[c, i], ydr.at[c, i], aside[i])
 
-    def query_side(c, i):
-        here = query.at[dp, piece(c)]
-        return remote(here, here, yqs.at[c, i], yqr.at[c, i], aside[i])
-
     for c in range(chunks):
 
         @pl.when(feeds)
         def _():
             mine[piece(c)] = x_ref[piece(c)].astype(jnp.bfloat16)
             feed(c, index).start()
-
-        @pl.when(is_query)
-        def _():
-            query[dp, piece(c)] = x_ref[piece(c)].astype(jnp.bfloat16)
-            query_hop(c).start()
-            for i in range(n_dp - 1):
-                query_side(c, i).start()
 
     for c in range(chunks):
 
@@ -360,16 +344,6 @@
         for i in range(n_dp - 1):
             doc_side(c, i).start()
 
-        @pl.when(jnp.logical_not(is_query))
-        def _():
-            query_hop(c).wait_recv()
-            for i in range(n_dp - 1):
-                query_side(c, i).start()
-
-        @pl.when(jnp.logical_and(grp > 0, grp < last))
-        def _():
-            query_hop(c).start()
-
     for c in range(chunks):
 
         @pl.when(feeds)
@@ -385,31 +359,23 @@
         def _():
             doc_hop(c, up, 0).wait_send()
 
-        @pl.when(grp > 0)
-        def _():
-            query_hop(c).wait_send()
-
         for i in range(n_dp - 1):
             doc_side(c, i).wait()
-            query_side(c, i).wait()
 
 
 def grads(x, n_grp, n_dp, chunks, collective):
     dma = pltpu.SemaphoreType.DMA
-    shape = jax.ShapeDtypeStruct((n_dp,) + x.shape, jnp.bfloat16)
     side = max(n_dp - 1, 1)
     return pl.pallas_call(
         functools.partial(grads_kernel, n_grp, n_dp, chunks),
-        out_shape=(shape, shape),
+        out_shape=jax.ShapeDtypeStruct((n_dp,) + x.shape, jnp.bfloat16),
         in_specs=[VMEM],
-        out_specs=(VMEM, VMEM),
+        out_specs=VMEM,
         scratch_shapes=[
             pltpu.VMEM(x.shape, jnp.bfloat16),
             pltpu.VMEM((n_grp - 2,) + x.shape, jnp.bfloat16),
             dma((chunks,)), dma((chunks, n_grp - 2)),
             dma((chunks, 2)), dma((chunks,)),
-            dma((chunks,)), dma((chunks,)),
-            dma((chunks, side)), dma((chunks, side)),
             dma((chunks, side)), dma((chunks, side)),
         ],
         compiler_params=params(collective),
@@ -444,6 +410,15 @@
     unit_rows = summed / row_norms
     embedded = unit_rows.astype(jnp.bfloat16)
     queries_all = gather(embedded, n_grp, n_dp, n_chip, 4, True, 1).reshape(-1, embed)
+    held, queries_all = lax.optimization_barrier((features, queries_all))
+    query_features = features
+    for g in range(n_grp - 1):
+        came = lax.ppermute(held, "grp", [(n_grp - 1, g)])
+        query_features = jnp.where(grp == g, came, query_features)
+    query_sides = [
+        lax.ppermute(query_features, "dp", [(i, (i + s) % n_dp) for i in range(n_dp)]) if s else query_features
+        for s in range(n_dp)
+    ]
     total_q = queries_all.shape[0]
     logits = inverse_temp * lax.dot_general(
         queries_all, embedded, (((1,), (1,)), ((), ())), preferred_element_type=jnp.float32
@@ -467,26 +442,32 @@
     dpassage = inverse_temp * lax.dot_general(
         dlogit, queries_all, (((0,), (0,)), ((), ())), preferred_element_type=jnp.float32
     )
-    grad_emb = jnp.where(is_query, dquery, dpassage)
-    inner = jnp.sum(unit_rows * grad_emb, axis=-1, keepdims=True)
-    grad_proj = ((grad_emb - unit_rows * inner) / row_norms).astype(jnp.bfloat16)
-    dy = gather(grad_proj, n_grp, n_dp, n_chip, 1, False, 4).reshape(n_dp, rows, embed)
-    grad_half = None
-    for s in range(n_dp):
-        term = lax.dot_general(
-            swapped[s],
-            lax.dynamic_index_in_dim(dy, lax.rem(dp + n_dp - s, n_dp), 0, keepdims=False),
-            (((0,), (0,)), ((), ())),
-            preferred_element_type=jnp.float32,
-        )
-        grad_half = term if grad_half is None else grad_half + term
-    doc16, query16 = grads(grad_half, n_grp, n_dp, 8, 5)
+
+    def back_norm(grad_emb):
+        inner = jnp.sum(unit_rows * grad_emb, axis=-1, keepdims=True)
+        return ((grad_emb - unit_rows * inner) / row_norms).astype(jnp.bfloat16)
+
+    def weight_grad(sides, dy):
+        total = None
+        for s in range(n_dp):
+            term = lax.dot_general(
+                sides[s],
+                lax.dynamic_index_in_dim(dy, lax.rem(dp + n_dp - s, n_dp), 0, keepdims=False),
+                (((0,), (0,)), ((), ())),
+                preferred_element_type=jnp.float32,
+            )
+            total = term if total is None else total + term
+        return total
+
+    dy = gather(back_norm(dpassage), n_grp, n_dp, n_chip, 1, False, 4).reshape(n_dp, rows, embed)
+    doc16 = grads(weight_grad(swapped, dy), n_grp, n_dp, 8, 5)
+    query_dy = gather(back_norm(dquery), n_grp, n_dp, n_chip, 4, True, 6).reshape(n_dp, rows, embed)
+    query_grad = weight_grad(query_sides, query_dy)
+    rows_dy = lax.dynamic_index_in_dim(jnp.where(is_query, query_dy, dy), dp, 0, keepdims=False)
     back = lax.dot_general(
-        lax.dynamic_index_in_dim(dy, dp, 0, keepdims=False), weight, (((1,), (1,)), ((), ())),
-        preferred_element_type=jnp.float32,
+        rows_dy, weight, (((1,), (1,)), ((), ())), preferred_element_type=jnp.float32
     ).astype(jnp.bfloat16)
     doc_grad = doc16.reshape(width, embed).astype(jnp.float32)
-    query_grad = query16.reshape(width, embed).astype(jnp.float32)
     return (loss, doc_grad, query_grad, back[None])
 
 

time: 245 us -> 275 us (1.12)
  Pallas kernels: 216 us -> 236 us
  matrix products: 13.3 us -> 20 us
  starting transfers between devices: 2.97 us -> 6.92 us
    pallas_call x1, Pallas kernels: 107 us -> 42.2 us  [grads(): pl.pallas_call(functools.partial(grads_kernel, n_grp, n_dp, chunks), out_...]
    pallas_call x1, Pallas kernels: 8.73 us -> 59.3 us  [stats(): pl.pallas_call(functools.partial(stats_kernel, n_grp, n_dp, n_mp), out_sh...]
    pallas_call x2 -> x3, Pallas kernels: 42.2 us -> 75.3 us  [gather(): pl.pallas_call(functools.partial(gather_kernel, n_grp, n_dp, n_chip, chun...]
    dot_general x3 -> x5, matrix products: 6.1 us -> 12.3 us  [the longest x4 9.99 us: weight_grad(): lax.dot_general(sides[s], lax.dynamic_index_in_dim(dy, lax.rem(dp + n_dp...]
    ppermute x0 -> x4, starting transfers between devices: none -> 5.45 us  [the longest x3 4.63 us: local(): came = lax.ppermute(held, 'grp', [(n_grp - 1, g)])]
  transfers between devices with their start and end apart: 1 -> 5, of which waited for: 0 -> 0; matrix products, arithmetic and copies ran while one was open for 5% -> 7% of each run, Pallas kernels for 45% -> 70%
where the time goes in v2:
time: 275 us
  Pallas kernels  236 us (86%)
  matrix products  20 us (7%)
  starting transfers between devices  6.92 us (3%)
  other arithmetic  5.81 us (2%)
  local copies, waits for them, and re-layouts  3.29 us (1%)
    pallas_call x3, Pallas kernels, gather(): pl.pallas_call(functools.partial(gather_kernel, n_grp, n_dp, n_chip, chun...  75.3 us
    pallas_call x2, Pallas kernels, scatter(): pl.pallas_call(functools.partial(scatter_kernel, n_grp, n_dp, n_chip, dow...  59.6 us
    pallas_call x1, Pallas kernels, stats(): pl.pallas_call(functools.partial(stats_kernel, n_grp, n_dp, n_mp), out_sh...  59.3 us
    pallas_call x1, Pallas kernels, grads(): pl.pallas_call(functools.partial(grads_kernel, n_grp, n_dp, chunks), out_...  42.2 us
    dot_general x4, matrix products, weight_grad(): lax.dot_general(sides[s], lax.dynamic_index_in_dim(dy, lax.rem(dp + n_dp...  9.99 us
  transfers between devices with their start and end apart: 5, of which 0 were waited for; matrix products, arithmetic and copies ran while one was open for 7% of the time, Pallas kernels for 70%

profile of v2, /device:TPU:0, one launch (start us, length us, event | category | flops | bytes accessed | tf_op | source)
XLA Modules:
  0.0 275.0 jit_solution(9189486009768022817)
XLA Ops:
  0.6 3.2 %fusion.15 = f32[1024,512]{0,1:T(8,128)S(1)} fusion(bf16[1024,1024]{1,0:T(8,128)(2,1)} %param.6, bf16[1024,1024]{1,0:T(8,128)(2,1)} %param.5, pred[]{:T(512)S(6)} %eq.25, bf16[1,512,1024]{2,1,0:T(8,128)(2,1)} %param.4), kind=kOutput, calls=%fused_computation.24 | convolution fusion | flops 1074790400 | bytes 7340033 | tf_op jit(solution)/shard_map/dot_general | solution.py:405
  3.8 17.3 %shard_map.75 = f32[128,1024]{1,0:T(8,128)S(1)} custom-call(f32[4,128,1024]{2,1,0:T(8,128)S(1)} %bitcast.58), custom_call_target="tpu_custom_call" | custom-call | tf_op jit(solution)/shard_map/pallas_call | solution.py:208
  21.1 0.1 multiply_reduce_fusion.2
  21.2 0.1 fusion.25.x_ref
  21.4 26.7 %shard_map.76 = bf16[8,128,1024]{2,1,0:T(8,128)(2,1)S(1)} custom-call(bf16[128,1024]{1,0:T(8,128)(2,1)S(1)} %fusion.25.x_ref), custom_call_target="tpu_custom_call" | custom-call | tf_op jit(solution)/shard_map/pallas_call | solution.py:121
  48.1 0.0 copy-start.2
  48.1 1.7 collective-permute-start.1
  49.7 1.7 collective-permute-start.2
  51.4 1.3 collective-permute-start.3
  52.7 1.9 dynamic-slice_bitcast_fusion
  54.6 1.5 collective-permute-start
  56.1 0.8 fusion.26
  57.0 0.2 exponential_reduce_fusion
  57.2 59.3 %shard_map.77 = f32[3,8,128]{2,1,0:T(8,128)S(1)} custom-call(f32[3,8,128]{2,1,0:T(8,128)S(1)} %pad_maximum_fusion.x_ref), custom_call_target="tpu_custom_call" | custom-call | tf_op jit(solution)/shard_map/pallas_call | solution.py:273
  116.5 0.6 fusion.23
  117.1 2.9 %convolution_multiply_fusion = f32[1024,1024]{1,0:T(8,128)} fusion(bf16[128,1024]{1,0:T(8,128)(2,1)S(1)} %fusion.25.x_ref, f32[1024,128]{0,1:T(8,128)S(1)} %get-tuple-element.17, f32[1024]{0:T(1024)S(1)} %get-tuple-element.14, s32[1024]{0:T(1024)S(1)} %copy-done.2, s32[128]{0:T(128)S(1)} %iota_add_fusion, pred[]{:T(512)S(6)} %not.3), kind=kOutput, calls=%fused_computation.1 | convolution fusion | flops 270663680 | bytes 4989441 | tf_op jit(solution)/shard_map/dot_general | solution.py:438
  120.0 42.3 %shard_map.80 = f32[128,1024]{1,0:T(8,128)S(1)} custom-call(f32[8,128,1024]{2,1,0:T(8,128)} %bitcast.59), custom_call_target="tpu_custom_call" | custom-call | tf_op jit(solution)/shard_map/pallas_call | solution.py:208
  162.3 0.8 multiply_reduce_fusion
  163.0 0.2 divide_convert_fusion
  163.3 32.1 %shard_map.81 = bf16[8,128,1024]{2,1,0:T(8,128)(2,1)S(1)} custom-call(bf16[128,1024]{1,0:T(8,128)(2,1)S(1)} %get-tuple-element.12.x_ref), custom_call_target="tpu_custom_call" | custom-call | tf_op jit(solution)/shard_map/pallas_call | solution.py:121
  195.4 16.5 %shard_map.78 = bf16[8,128,1024]{2,1,0:T(8,128)(2,1)S(1)} custom-call(bf16[128,1024]{1,0:T(8,128)(2,1)S(1)} %get-tuple-element.13.x_ref), custom_call_target="tpu_custom_call" | custom-call | tf_op jit(solution)/shard_map/pallas_call | solution.py:121
  211.9 1.3 copy-done
  213.9 2.3 fusion.8
  216.2 1.9 select_select_fusion
  218.1 0.8 collective-permute-start.4
  218.9 0.1 copy-done.3
  219.0 2.3 fusion
  221.3 3.1 %convolution_add_fusion.1.x_ref = f32[512,1024]{1,0:T(8,128)} fusion(f32[512,1024]{1,0:T(8,128)S(1)} %fusion.8, bf16[512,512]{1,0:T(8,128)(2,1)} %collective-permute-done, bf16[2,512,1024]{2,1,0:T(8,128)(2,1)S(1)} %bitcast.57, s32[]{:T(128)S(6)} %select_n.115), kind=kOutput, calls=%fused_computation.4 | convolution fusion | flops 537395200 | bytes 5767172 | tf_op jit(solution)/shard_map/dot_general | solution.py:453
  224.5 42.2 %shard_map.79 = bf16[2,512,1024]{2,1,0:T(8,128)(2,1)S(1)} custom-call(f32[512,1024]{1,0:T(8,128)} %convolution_add_fusion.1.x_ref), custom_call_target="tpu_custom_call" | custom-call | tf_op jit(solution)/shard_map/pallas_call | solution.py:369
  266.6 2.6 bitcast_convert_fusion
  269.3 1.3 fusion.4
  270.6 3.3 %convolution_add_fusion = f32[1024,1024]{1,0:T(8,128)} fusion(f32[1024,1024]{1,0:T(8,128)S(1)} %fusion.4, bf16[512,1024]{1,0:T(8,128)(2,1)S(1)} %select_select_fusion, bf16[2,512,1024]{2,1,0:T(8,128)(2,1)S(1)} %bitcast.52, s32[]{:T(128)S(6)} %select_n.113), kind=kOutput, calls=%fused_computation | convolution fusion | flops 1074790400 | bytes 10485764 | tf_op jit(solution)/shard_map/dot_general | solution.py:453
  (16 shorter events, 0.1 us)
Async XLA Ops:
  48.1 8.9 %copy-start.2 = (s32[1024]{0:T(1024)S(1)}, s32[1024]{0:T(1024)}, u32[]{:S(2)}) copy-start(s32[1024]{0:T(1024)} %param.7) | copy-start | bytes 12292
  48.1 168.1 %collective-permute-start.1 = (bf16[512,1024]{1,0:T(8,128)(2,1)}, bf16[512,1024]{1,0:T(8,128)(2,1)}, u32[]{:S(2)}, u32[]{:S(2)}) collective-permute-start(bf16[512,1024]{1,0:T(8,128)(2,1)} %bitcast), channel_id=1, source_target_pairs={{24,16},{25,17},{26,18},{27,19},{28,20},{29,21},{30,22},{31,23}} | collective-permute-start | bytes 3145736 | tf_op jit(solution)/shard_map/ppermute | solution.py:416
  49.7 166.5 %collective-permute-start.2 = (bf16[512,1024]{1,0:T(8,128)(2,1)}, bf16[512,1024]{1,0:T(8,128)(2,1)}, u32[]{:S(2)}, u32[]{:S(2)}) collective-permute-start(bf16[512,1024]{1,0:T(8,128)(2,1)} %bitcast), channel_id=1, source_target_pairs={{24,8},{25,9},{26,10},{27,11},{28,12},{29,13},{30,14},{31,15}} | collective-permute-start | bytes 3145736 | tf_op jit(solution)/shard_map/ppermute | solution.py:416
  51.4 164.8 %collective-permute-start.3 = (bf16[512,1024]{1,0:T(8,128)(2,1)}, bf16[512,1024]{1,0:T(8,128)(2,1)}, u32[]{:S(2)}, u32[]{:S(2)}) collective-permute-start(bf16[512,1024]{1,0:T(8,128)(2,1)} %bitcast), channel_id=1, source_target_pairs={{24,0},{25,1},{26,2},{27,3},{28,4},{29,5},{30,6},{31,7}} | collective-permute-start | bytes 3145736 | tf_op jit(solution)/shard_map/ppermute | solution.py:416
  54.6 166.8 %collective-permute-start = (bf16[512,512]{1,0:T(8,128)(2,1)}, bf16[512,512]{1,0:T(8,128)(2,1)}, u32[]{:S(2)}, u32[]{:S(2)}) collective-permute-start(bf16[512,512]{1,0:T(8,128)(2,1)} %dynamic-slice_bitcast_fusion), channel_id=1, source_target_pairs={{0,4},{4,0},{1,5},{5,1},{2,6},{6,2},{3,7},{7,3},{8,12},{12,8},{9,1... | collective-permute-start | bytes 1572872 | tf_op jit(solution)/shard_map/ppermute | solution.py:401
  211.9 1.3 copy-start
  213.9 5.1 %copy-start.4 = (bf16[1024,1024]{1,0:T(8,128)(2,1)S(1)}, bf16[1024,1024]{1,0:T(8,128)(2,1)}, u32[]{:S(2)}) copy-start(bf16[1024,1024]{1,0:T(8,128)(2,1)} %param.5) | copy-start | bytes 6291460
  216.1 2.8 %copy-start.1 = (bf16[8,128,1024]{2,1,0:T(8,128)(2,1)S(1)}, bf16[8,128,1024]{2,1,0:T(8,128)(2,1)}, u32[]{:S(2)}) copy-start(bf16[8,128,1024]{2,1,0:T(8,128)(2,1)} %copy-done) | copy-start | bytes 6291460
  216.2 2.8 %copy-start.3 = (bf16[1024,1024]{1,0:T(8,128)(2,1)S(1)}, bf16[1024,1024]{1,0:T(8,128)(2,1)}, u32[]{:S(2)}) copy-start(bf16[1024,1024]{1,0:T(8,128)(2,1)} %param.6) | copy-start | bytes 6291460
  218.1 51.2 %collective-permute-start.4 = (bf16[512,1024]{1,0:T(8,128)(2,1)S(1)}, bf16[512,1024]{1,0:T(8,128)(2,1)S(1)}, u32[]{:S(2)}, u32[]{:S(2)}) collective-permute-start(bf16[512,1024]{1,0:T(8,128)(2,1)S(1)} %select_select_fusion), channel_id=1, source_target_pairs={{0,4},{4,0},{1,5},{5,1},{2,6},{6,2},{3,7},{7,3},{8,12},{12,8},{9,1... | collective-permute-start | bytes 3145736 | tf_op jit(solution)/shard_map/ppermute | solution.py:419

commit v3 on v2

--- a/solution.py
+++ b/solution.py
@@ -11,7 +11,7 @@
 epsilon_norm = 1e-06
 MESH = pl.DeviceIdType.MESH
 VMEM = pl.BlockSpec(memory_space=pltpu.VMEM)
-LIMIT = 50 * 1024 * 1024
+LIMIT = 56 * 1024 * 1024
 
 
 def place():
@@ -132,7 +132,7 @@
     )(x)
 
 
-def scatter_kernel(n_grp, n_dp, n_chip, down, steps, x_ref, out_ref, near, far_out, far, zbuf, ns, nr, fs, fr, zs, zr):
+def scatter_steps(n_grp, n_dp, n_chip, down, steps, x_ref, out_ref, near, far_out, far, zbuf, ns, nr, fs, fr, zs, zr):
     grp, dp, chip, core = place()
     offsets = [(d, k) for d in range(n_dp) for k in range(n_chip)]
     offsets = offsets[1:] + offsets[:1]
@@ -150,12 +150,13 @@
     targets = [sibling] + [peer(d, k) for d, k in offsets[:-1]]
     if down:
         targets += [{"grp": lax.rem(grp + 1, n_grp)}, {"grp": lax.rem(grp + n_grp - 1, n_grp)}]
-    meet(targets)
+    yield targets
     first = []
     for i, (d, k) in enumerate(offsets):
         copy = remote(x_ref.at[slot(d, k, 1 - core)], near.at[i], ns.at[i], nr.at[i], sibling)
         copy.start()
         first.append(copy)
+    yield None
     second = []
     for i, (d, k) in enumerate(offsets[:-1]):
         first[i].wait_recv()
@@ -163,6 +164,7 @@
         copy = remote(far_out.at[i], far.at[i], fs.at[i], fr.at[i], peer(d, k))
         copy.start()
         second.append(copy)
+    yield None
     first[-1].wait_recv()
     total = x_ref[slot(0, 0, core)] + near[len(offsets) - 1]
     for i, copy in enumerate(second):
@@ -199,26 +201,36 @@
                 hop(c).wait_send()
 
 
-def scatter(x, n_grp, n_dp, n_chip, wire, down, collective):
+def scatter_kernel(n_grp, n_dp, n_chip, *refs):
+    steps = scatter_steps(n_grp, n_dp, n_chip, False, 8, *refs)
+    meet(next(steps))
+    for _ in steps:
+        pass
+
+
+def scatter_scratch(block, n_grp, n_dp, n_chip, wire, down):
     count = n_dp * n_chip
+    peers = max(count - 1, 1)
+    dma = pltpu.SemaphoreType.DMA
+    return [
+        pltpu.VMEM((count,) + block, jnp.float32),
+        pltpu.VMEM((peers,) + block, wire),
+        pltpu.VMEM((peers,) + block, wire),
+        pltpu.VMEM(block if down else (16, 128), jnp.float32),
+        dma((count,)), dma((count,)),
+        dma((peers,)), dma((peers,)),
+        dma((8,)), dma((8,)),
+    ]
+
+
+def scatter(x, n_grp, n_dp, n_chip, wire, collective):
     block = x.shape[1:]
-    dma = pltpu.SemaphoreType.DMA
-    z_block = block if down else (16, 128)
-    peers = max(count - 1, 1)
     return pl.pallas_call(
-        functools.partial(scatter_kernel, n_grp, n_dp, n_chip, down, 8),
+        functools.partial(scatter_kernel, n_grp, n_dp, n_chip),
         out_shape=jax.ShapeDtypeStruct(block, jnp.float32),
         in_specs=[VMEM],
         out_specs=VMEM,
-        scratch_shapes=[
-            pltpu.VMEM((count,) + block, jnp.float32),
-            pltpu.VMEM((peers,) + block, wire),
-            pltpu.VMEM((peers,) + block, wire),
-            pltpu.VMEM(z_block, jnp.float32),
-            dma((count,)), dma((count,)),
-            dma((peers,)), dma((peers,)),
-            dma((8,)), dma((8,)),
-        ],
+        scratch_shapes=scatter_scratch(block, n_grp, n_dp, n_chip, wire, False),
         compiler_params=params(collective),
     )(x)
 
@@ -286,7 +298,7 @@
     )(x)
 
 
-def grads_kernel(n_grp, n_dp, chunks, x_ref, doc, mine, parts, ps, pr, ds, dr, yds, ydr):
+def grads_steps(n_grp, n_dp, chunks, x_ref, doc, mine, parts, ps, pr, ds, dr, yds, ydr):
     grp, dp = lax.axis_index("grp"), lax.axis_index("dp")
     last = n_grp - 1
     root = 1
@@ -294,7 +306,7 @@
     up = {"grp": lax.rem(grp + 1, n_grp)}
     under = {"grp": lax.rem(grp + n_grp - 1, n_grp)}
     aside = [{"dp": lax.rem(dp + d, n_dp)} for d in range(1, n_dp)]
-    meet([{"grp": lax.rem(grp + i, n_grp)} for i in range(1, n_grp)] + aside)
+    yield [{"grp": lax.rem(grp + i, n_grp)} for i in range(1, n_grp)] + aside
     is_root = grp == root
     feeds = jnp.logical_and(jnp.logical_not(is_root), grp < last)
     others = [g for g in range(last) if g != root]
@@ -321,6 +333,7 @@
             mine[piece(c)] = x_ref[piece(c)].astype(jnp.bfloat16)
             feed(c, index).start()
 
+    yield None
     for c in range(chunks):
 
         @pl.when(is_root)
@@ -344,6 +357,8 @@
         for i in range(n_dp - 1):
             doc_side(c, i).start()
 
+        yield None
+
     for c in range(chunks):
 
         @pl.when(feeds)
@@ -363,23 +378,83 @@
             doc_side(c, i).wait()
 
 
-def grads(x, n_grp, n_dp, chunks, collective):
+def feature_steps(n_grp, chunks, f_ref, qf_ref, send, recv):
+    grp = lax.axis_index("grp")
+    last = grp == n_grp - 1
+    rows = f_ref.shape[0] // chunks
+    under = {"grp": lax.rem(grp + n_grp - 1, n_grp)}
+    yield [{"grp": lax.rem(grp + 1, n_grp)}, under]
+
+    def hop(c, source):
+        piece = pl.ds(c * rows, rows)
+        return remote(source.at[piece], qf_ref.at[piece], send.at[c], recv.at[c], under)
+
+    @pl.when(last)
+    def _():
+        for c in range(chunks):
+            hop(c, f_ref).start()
+        qf_ref[...] = f_ref[...]
+
+    yield None
+    for c in range(chunks):
+
+        @pl.when(jnp.logical_not(last))
+        def _():
+            hop(c, qf_ref).wait_recv()
+
+        @pl.when(jnp.logical_and(grp > 0, jnp.logical_not(last)))
+        def _():
+            hop(c, qf_ref).start()
+
+        yield None
+
+    for c in range(chunks):
+
+        @pl.when(grp > 0)
+        def _():
+            hop(c, qf_ref).wait_send()
+
+
+def back_kernel(n_grp, n_dp, n_chip, chunks, x_ref, f_ref, g_ref, out_ref, qf_ref, doc_ref, *scratch):
+    sums = scatter_steps(n_grp, n_dp, n_chip, True, 8, x_ref, out_ref, *scratch[:10])
+    docs = grads_steps(n_grp, n_dp, chunks, g_ref, doc_ref, *scratch[10:18])
+    ways = feature_steps(n_grp, chunks, f_ref, qf_ref, *scratch[18:])
+    meet(next(sums) + next(docs) + next(ways))
+    next(sums)
+    next(ways)
+    next(docs)
+    next(sums)
+    for c in range(chunks):
+        next(ways)
+        next(docs)
+    for steps in (sums, ways, docs):
+        for _ in steps:
+            pass
+
+
+def back_sums(x, features, g, n_grp, n_dp, n_chip, chunks, collective):
     dma = pltpu.SemaphoreType.DMA
     side = max(n_dp - 1, 1)
+    block = x.shape[1:]
     return pl.pallas_call(
-        functools.partial(grads_kernel, n_grp, n_dp, chunks),
-        out_shape=jax.ShapeDtypeStruct((n_dp,) + x.shape, jnp.bfloat16),
-        in_specs=[VMEM],
-        out_specs=VMEM,
-        scratch_shapes=[
-            pltpu.VMEM(x.shape, jnp.bfloat16),
-            pltpu.VMEM((n_grp - 2,) + x.shape, jnp.bfloat16),
+        functools.partial(back_kernel, n_grp, n_dp, n_chip, chunks),
+        out_shape=(
+            jax.ShapeDtypeStruct(block, jnp.float32),
+            jax.ShapeDtypeStruct(features.shape, features.dtype),
+            jax.ShapeDtypeStruct((n_dp,) + g.shape, jnp.bfloat16),
+        ),
+        in_specs=[VMEM] * 3,
+        out_specs=(VMEM,) * 3,
+        scratch_shapes=scatter_scratch(block, n_grp, n_dp, n_chip, jnp.float32, True) + [
+            pltpu.VMEM(g.shape, jnp.bfloat16),
+            pltpu.VMEM((n_grp - 2,) + g.shape, jnp.bfloat16),
             dma((chunks,)), dma((chunks, n_grp - 2)),
             dma((chunks, 2)), dma((chunks,)),
             dma((chunks, side)), dma((chunks, side)),
+            dma((chunks,)), dma((chunks,)),
         ],
         compiler_params=params(collective),
-    )(x)
+    )(x, features, g)
 
 
 def local(tower_features, doc_weight, query_weight, positive_ids):
@@ -404,21 +479,12 @@
     weight = jnp.where(is_query, query_weight, doc_weight)
     projected = jnp.dot(features, weight, preferred_element_type=jnp.float32)
     summed = scatter(
-        projected.reshape(n_mp, per_device, embed), n_grp, 1, n_chip, jnp.float32, False, 0
+        projected.reshape(n_mp, per_device, embed), n_grp, 1, n_chip, jnp.float32, 0
     )
     row_norms = jnp.sqrt(jnp.sum(summed * summed, axis=-1, keepdims=True) + epsilon_norm)
     unit_rows = summed / row_norms
     embedded = unit_rows.astype(jnp.bfloat16)
     queries_all = gather(embedded, n_grp, n_dp, n_chip, 4, True, 1).reshape(-1, embed)
-    held, queries_all = lax.optimization_barrier((features, queries_all))
-    query_features = features
-    for g in range(n_grp - 1):
-        came = lax.ppermute(held, "grp", [(n_grp - 1, g)])
-        query_features = jnp.where(grp == g, came, query_features)
-    query_sides = [
-        lax.ppermute(query_features, "dp", [(i, (i + s) % n_dp) for i in range(n_dp)]) if s else query_features
-        for s in range(n_dp)
-    ]
     total_q = queries_all.shape[0]
     logits = inverse_temp * lax.dot_general(
         queries_all, embedded, (((1,), (1,)), ((), ())), preferred_element_type=jnp.float32
@@ -436,9 +502,6 @@
     probs = jnp.where(passage_live, jnp.exp(jnp.where(passage_live, logits - lse[:, None], 0.0)), 0.0)
     dlogit = ((probs - positive_hit.astype(jnp.float32)) / total_q).astype(jnp.bfloat16)
     dq_part = inverse_temp * jnp.dot(dlogit, embedded, preferred_element_type=jnp.float32)
-    dquery = scatter(
-        dq_part.reshape(n_dp * n_mp, per_device, embed), n_grp, n_dp, n_chip, jnp.float32, True, 3
-    )
     dpassage = inverse_temp * lax.dot_general(
         dlogit, queries_all, (((0,), (0,)), ((), ())), preferred_element_type=jnp.float32
     )
@@ -460,7 +523,14 @@
         return total
 
     dy = gather(back_norm(dpassage), n_grp, n_dp, n_chip, 1, False, 4).reshape(n_dp, rows, embed)
-    doc16 = grads(weight_grad(swapped, dy), n_grp, n_dp, 8, 5)
+    dquery, query_features, doc16 = back_sums(
+        dq_part.reshape(n_dp * n_mp, per_device, embed), features, weight_grad(swapped, dy),
+        n_grp, n_dp, n_chip, 8, 3,
+    )
+    query_sides = [
+        lax.ppermute(query_features, "dp", [(i, (i + s) % n_dp) for i in range(n_dp)]) if s else query_features
+        for s in range(n_dp)
+    ]
     query_dy = gather(back_norm(dquery), n_grp, n_dp, n_chip, 4, True, 6).reshape(n_dp, rows, embed)
     query_grad = weight_grad(query_sides, query_dy)
     rows_dy = lax.dynamic_index_in_dim(jnp.where(is_query, query_dy, dy), dp, 0, keepdims=False)

time: 275 us -> 277 us (level)
  Pallas kernels: 236 us -> 215 us
  waiting for transfers between devices: 0.01 us -> 14.9 us
  other arithmetic: 5.81 us -> 12 us
  matrix products: 20 us -> 24 us
    pallas_call x1, Pallas kernels: 59.3 us -> 10 us  [stats(): pl.pallas_call(functools.partial(stats_kernel, n_grp, n_dp, n_mp), out_sh...]
    pallas_call x3 -> x2, Pallas kernels: 102 us -> 125 us  [the longest x1 106 us: back_sums(): pl.pallas_call(functools.partial(back_kernel, n_grp, n_dp, n_chip, chunks...]
    ppermute x1, waiting for transfers between devices: 0.01 us -> 14.9 us  [local(): lax.ppermute(query_features, 'dp', [(i, (i + s) % n_dp) for i in range(n_...]
    pallas_call x3, Pallas kernels: 75.3 us -> 80.7 us  [gather(): pl.pallas_call(functools.partial(gather_kernel, n_grp, n_dp, n_chip, chun...]
    ppermute x3 -> x0, starting transfers between devices: 4.63 us -> none  [local(): came = lax.ppermute(held, 'grp', [(n_grp - 1, g)])]
  transfers between devices with their start and end apart: 5 -> 2, of which waited for: 0 -> 1; matrix products, arithmetic and copies ran while one was open for 7% -> 10% of each run, Pallas kernels for 70% -> 27%
where the time goes in v3:
time: 277 us
  Pallas kernels  215 us (78%)
  matrix products  24 us (9%)
  waiting for transfers between devices  14.9 us (5%)
  other arithmetic  12 us (4%)
  starting transfers between devices  4.2 us (2%)
  local copies, waits for them, and re-layouts  3.52 us (1%)
    pallas_call x1, Pallas kernels, back_sums(): pl.pallas_call(functools.partial(back_kernel, n_grp, n_dp, n_chip, chunks...  106 us
    pallas_call x3, Pallas kernels, gather(): pl.pallas_call(functools.partial(gather_kernel, n_grp, n_dp, n_chip, chun...  80.7 us
    pallas_call x1, Pallas kernels, scatter(): pl.pallas_call(functools.partial(scatter_kernel, n_grp, n_dp, n_chip), ou...  18.7 us
    ppermute x1, waiting for transfers between devices, local(): lax.ppermute(query_features, 'dp', [(i, (i + s) % n_dp) for i in range(n_...  14.9 us
    dot_general x4, matrix products, weight_grad(): lax.dot_general(sides[s], lax.dynamic_index_in_dim(dy, lax.rem(dp + n_dp...  11.1 us
    pallas_call x1, Pallas kernels, stats(): pl.pallas_call(functools.partial(stats_kernel, n_grp, n_dp, n_mp), out_sh...  10 us
  transfers between devices with their start and end apart: 2, of which 1 were waited for; matrix products, arithmetic and copies ran while one was open for 10% of the time, Pallas kernels for 27%

profile of v3, /device:TPU:0, one launch (start us, length us, event | category | flops | bytes accessed | tf_op | source)
XLA Modules:
  0.0 276.5 jit_solution(5114057664205826716)
XLA Ops:
  0.6 1.9 dynamic-slice_bitcast_fusion
  2.5 3.0 %collective-permute-start = (bf16[512,512]{1,0:T(8,128)(2,1)}, bf16[512,512]{1,0:T(8,128)(2,1)}, u32[]{:S(2)}, u32[]{:S(2)}) collective-permute-start(bf16[512,512]{1,0:T(8,128)(2,1)} %dynamic-slice_bitcast_fusion), channel_id=1, source_target_pairs={{0,4},{4,0},{1,5},{5,1},{2,6},{6,2},{3,7},{7,3},{8,12},{12,8},{9,1... | collective-permute-start | bytes 1572872 | tf_op jit(solution)/shard_map/ppermute | solution.py:476
  5.5 4.5 %fusion.15 = f32[1024,512]{0,1:T(8,128)} fusion(bf16[1024,1024]{1,0:T(8,128)(2,1)} %param.6, bf16[1024,1024]{1,0:T(8,128)(2,1)} %param.5, pred[]{:T(512)S(6)} %eq.16, bf16[1,512,1024]{2,1,0:T(8,128)(2,1)} %param.4), kind=kOutput, calls=%fused_computation.23 | convolution fusion | flops 1074790400 | bytes 7340033 | tf_op jit(solution)/shard_map/dot_general | solution.py:480
  10.0 18.7 %shard_map.75 = f32[128,1024]{1,0:T(8,128)} custom-call(f32[4,128,1024]{2,1,0:T(8,128)} %bitcast.59), custom_call_target="tpu_custom_call" | custom-call | tf_op jit(solution)/shard_map/pallas_call | solution.py:228
  28.7 1.2 multiply_reduce_fusion.2
  29.9 1.9 fusion.25.x_ref
  31.8 28.5 %shard_map.76 = bf16[8,128,1024]{2,1,0:T(8,128)(2,1)} custom-call(bf16[128,1024]{1,0:T(8,128)(2,1)} %fusion.25.x_ref), custom_call_target="tpu_custom_call" | custom-call | tf_op jit(solution)/shard_map/pallas_call | solution.py:121
  60.2 2.6 fusion.26
  62.9 0.2 exponential_reduce_fusion
  63.1 0.6 pad_maximum_fusion.x_ref
  63.7 10.0 %shard_map.77 = f32[3,8,128]{2,1,0:T(8,128)} custom-call(f32[3,8,128]{2,1,0:T(8,128)} %pad_maximum_fusion.x_ref), custom_call_target="tpu_custom_call" | custom-call | tf_op jit(solution)/shard_map/pallas_call | solution.py:285
  73.7 1.3 fusion.23
  75.0 0.7 multiply_reduce_fusion.1
  75.7 0.9 divide_convert_fusion.1.x_ref
  76.6 18.1 %shard_map.78 = bf16[8,128,1024]{2,1,0:T(8,128)(2,1)} custom-call(bf16[128,1024]{1,0:T(8,128)(2,1)} %divide_convert_fusion.1.x_ref), custom_call_target="tpu_custom_call" | custom-call | tf_op jit(solution)/shard_map/pallas_call | solution.py:121
  95.4 2.0 fusion.8
  97.3 2.9 %convolution_multiply_fusion = f32[1024,1024]{1,0:T(8,128)} fusion(bf16[128,1024]{1,0:T(8,128)(2,1)S(1)} %copy-done.5, f32[1024,128]{0,1:T(8,128)S(1)} %get-tuple-element.15, f32[1024]{0:T(1024)S(1)} %get-tuple-element.12, s32[1024]{0:T(1024)S(1)} %copy-done.8, s32[128]{0:T(128)S(1)} %iota_add_fusion, pred[]{:T(512)S(6)} %not.3), kind=kOutput, calls=%fused_computation.1 | convolution fusion | flops 270663680 | bytes 4989441 | tf_op jit(solution)/shard_map/dot_general | solution.py:504
  100.2 3.1 %convolution_add_fusion.1.g_ref = f32[512,1024]{1,0:T(8,128)} fusion(f32[512,1024]{1,0:T(8,128)S(1)} %fusion.8, bf16[512,512]{1,0:T(8,128)(2,1)} %collective-permute-done, bf16[2,512,1024]{2,1,0:T(8,128)(2,1)S(1)} %bitcast.54, s32[]{:T(128)S(6)} %select_n.95), kind=kOutput, calls=%fused_computation.4 | convolution fusion | flops 537395200 | bytes 5767172 | tf_op jit(solution)/shard_map/dot_general | solution.py:516
  103.3 105.8 %shard_map.79 = (f32[128,1024]{1,0:T(8,128)}, bf16[512,1024]{1,0:T(8,128)(2,1)}, bf16[2,512,1024]{2,1,0:T(8,128)(2,1)}) custom-call(f32[8,128,1024]{2,1,0:T(8,128)} %bitcast.49, bf16[512,1024]{1,0:T(8,128)(2,1)} %bitcast.58, f32[512,1024]{1,0:T(8,128)} %convolution_add_fusion.1.g_ref), custom_call_target="tpu_custom_call" | custom-call | tf_op jit(solution)/shard_map/pallas_call | solution.py:439
  209.1 1.2 multiply_reduce_fusion
  210.4 2.0 divide_convert_fusion.x_ref
  212.4 34.2 %shard_map.80 = bf16[8,128,1024]{2,1,0:T(8,128)(2,1)} custom-call(bf16[128,1024]{1,0:T(8,128)(2,1)} %divide_convert_fusion.x_ref), custom_call_target="tpu_custom_call" | custom-call | tf_op jit(solution)/shard_map/pallas_call | solution.py:121
  246.6 1.2 collective-permute-start.1
  247.8 2.7 fusion.5
  250.5 0.0 copy-start.9
  250.5 0.0 copy-start.10
  250.5 2.7 bitcast_convert_fusion
  253.3 1.0 copy-done.9
  254.2 0.6 copy-done.10
  254.9 2.3 fusion
  257.1 14.9 %collective-permute-done.1 = bf16[512,1024]{1,0:T(8,128)(2,1)S(1)} collective-permute-done((bf16[512,1024]{1,0:T(8,128)(2,1)S(1)}, bf16[512,1024]{1,0:T(8,128)(2,1)S(1)}, u32[]{:S(2)}, u32[]{:S(2)}) %collective-permute-start.1) | collective-permute-done | bytes 1048608 | tf_op jit(solution)/shard_map/ppermute | solution.py:531
  272.0 3.4 %convolution_add_fusion = f32[1024,1024]{1,0:T(8,128)} fusion(f32[1024,1024]{1,0:T(8,128)S(1)} %fusion.5, bf16[512,1024]{1,0:T(8,128)(2,1)S(1)} %collective-permute-done.1, bf16[2,512,1024]{2,1,0:T(8,128)(2,1)S(1)} %bitcast.52, s32[]{:T(128)S(6)} %select_n.95), kind=kOutput, calls=%fused_computation | convolution fusion | flops 1074790400 | bytes 10485764 | tf_op jit(solution)/shard_map/dot_general | solution.py:516
  (22 shorter events, 0.1 us)
Async XLA Ops:
  2.5 97.7 %collective-permute-start = (bf16[512,512]{1,0:T(8,128)(2,1)}, bf16[512,512]{1,0:T(8,128)(2,1)}, u32[]{:S(2)}, u32[]{:S(2)}) collective-permute-start(bf16[512,512]{1,0:T(8,128)(2,1)} %dynamic-slice_bitcast_fusion), channel_id=1, source_target_pairs={{0,4},{4,0},{1,5},{5,1},{2,6},{6,2},{3,7},{7,3},{8,12},{12,8},{9,1... | collective-permute-start | bytes 1572872 | tf_op jit(solution)/shard_map/ppermute | solution.py:476
  31.7 28.5 %copy-start.5 = (bf16[128,1024]{1,0:T(8,128)(2,1)S(1)}, bf16[128,1024]{1,0:T(8,128)(2,1)}, u32[]{:S(2)}) copy-start(bf16[128,1024]{1,0:T(8,128)(2,1)} %fusion.25.x_ref) | copy-start | bytes 786436
  31.7 31.1 %copy-start.8 = (s32[1024]{0:T(1024)S(1)}, s32[1024]{0:T(1024)}, u32[]{:S(2)}) copy-start(s32[1024]{0:T(1024)} %param.7) | copy-start | bytes 12292
  60.2 14.8 %copy-start = (f32[128,1024]{1,0:T(8,128)S(1)}, f32[128,1024]{1,0:T(8,128)}, u32[]{:S(2)}) copy-start(f32[128,1024]{1,0:T(8,128)} %shard_map.75) | copy-start | bytes 1572868
  60.2 14.8 %copy-start.3 = (bf16[8,128,1024]{2,1,0:T(8,128)(2,1)S(1)}, bf16[8,128,1024]{2,1,0:T(8,128)(2,1)}, u32[]{:S(2)}) copy-start(bf16[8,128,1024]{2,1,0:T(8,128)(2,1)} %shard_map.76) | copy-start | bytes 6291460
  75.7 19.6 %copy-start.4 = (bf16[1,512,1024]{2,1,0:T(8,128)(2,1)S(1)}, bf16[1,512,1024]{2,1,0:T(8,128)(2,1)}, u32[]{:S(2)}) copy-start(bf16[1,512,1024]{2,1,0:T(8,128)(2,1)} %param.4) | copy-start | bytes 3145732
  97.3 2.9 %copy-start.2 = (bf16[8,128,1024]{2,1,0:T(8,128)(2,1)S(1)}, bf16[8,128,1024]{2,1,0:T(8,128)(2,1)}, u32[]{:S(2)}) copy-start(bf16[8,128,1024]{2,1,0:T(8,128)(2,1)} %shard_map.78) | copy-start | bytes 6291460
  210.4 36.2 %copy-start.7 = (bf16[512,1024]{1,0:T(8,128)(2,1)S(1)}, bf16[512,1024]{1,0:T(8,128)(2,1)}, u32[]{:S(2)}) copy-start(bf16[512,1024]{1,0:T(8,128)(2,1)} %get-tuple-element.8) | copy-start | bytes 3145732
  246.6 25.5 %collective-permute-start.1 = (bf16[512,1024]{1,0:T(8,128)(2,1)S(1)}, bf16[512,1024]{1,0:T(8,128)(2,1)S(1)}, u32[]{:S(2)}, u32[]{:S(2)}) collective-permute-start(bf16[512,1024]{1,0:T(8,128)(2,1)S(1)} %copy-done.7), channel_id=1, source_target_pairs={{0,4},{4,0},{1,5},{5,1},{2,6},{6,2},{3,7},{7,3},{8,12},{12,8},{9,1... | collective-permute-start | bytes 3145736 | tf_op jit(solution)/shard_map/ppermute | solution.py:531
  247.8 2.7 copy-start.6
  250.5 2.8 %copy-start.1 = (bf16[8,128,1024]{2,1,0:T(8,128)(2,1)S(1)}, bf16[8,128,1024]{2,1,0:T(8,128)(2,1)}, u32[]{:S(2)}) copy-start(bf16[8,128,1024]{2,1,0:T(8,128)(2,1)} %shard_map.80) | copy-start | bytes 6291460
  250.5 3.7 %copy-start.9 = (bf16[1024,1024]{1,0:T(8,128)(2,1)S(1)}, bf16[1024,1024]{1,0:T(8,128)(2,1)}, u32[]{:S(2)}) copy-start(bf16[1024,1024]{1,0:T(8,128)(2,1)} %param.6) | copy-start | bytes 6291460
  250.5 4.4 %copy-start.10 = (bf16[1024,1024]{1,0:T(8,128)(2,1)S(1)}, bf16[1024,1024]{1,0:T(8,128)(2,1)}, u32[]{:S(2)}) copy-start(bf16[1024,1024]{1,0:T(8,128)(2,1)} %param.5) | copy-start | bytes 6291460

commit v4 on v3

--- a/solution.py
+++ b/solution.py
@@ -11,7 +11,7 @@
 epsilon_norm = 1e-06
 MESH = pl.DeviceIdType.MESH
 VMEM = pl.BlockSpec(memory_space=pltpu.VMEM)
-LIMIT = 56 * 1024 * 1024
+LIMIT = 50 * 1024 * 1024
 
 
 def place():
@@ -415,46 +415,62 @@
             hop(c, qf_ref).wait_send()
 
 
-def back_kernel(n_grp, n_dp, n_chip, chunks, x_ref, f_ref, g_ref, out_ref, qf_ref, doc_ref, *scratch):
+def back_kernel(n_grp, n_dp, n_chip, chunks, x_ref, f_ref, out_ref, qf_ref, *scratch):
     sums = scatter_steps(n_grp, n_dp, n_chip, True, 8, x_ref, out_ref, *scratch[:10])
-    docs = grads_steps(n_grp, n_dp, chunks, g_ref, doc_ref, *scratch[10:18])
-    ways = feature_steps(n_grp, chunks, f_ref, qf_ref, *scratch[18:])
-    meet(next(sums) + next(docs) + next(ways))
+    ways = feature_steps(n_grp, chunks, f_ref, qf_ref, *scratch[10:])
+    meet(next(sums) + next(ways))
     next(sums)
     next(ways)
-    next(docs)
     next(sums)
     for c in range(chunks):
         next(ways)
-        next(docs)
-    for steps in (sums, ways, docs):
+    for steps in (sums, ways):
         for _ in steps:
             pass
 
 
-def back_sums(x, features, g, n_grp, n_dp, n_chip, chunks, collective):
+def back_sums(x, features, n_grp, n_dp, n_chip, chunks, collective):
     dma = pltpu.SemaphoreType.DMA
-    side = max(n_dp - 1, 1)
     block = x.shape[1:]
     return pl.pallas_call(
         functools.partial(back_kernel, n_grp, n_dp, n_chip, chunks),
         out_shape=(
             jax.ShapeDtypeStruct(block, jnp.float32),
             jax.ShapeDtypeStruct(features.shape, features.dtype),
-            jax.ShapeDtypeStruct((n_dp,) + g.shape, jnp.bfloat16),
         ),
-        in_specs=[VMEM] * 3,
-        out_specs=(VMEM,) * 3,
+        in_specs=[VMEM] * 2,
+        out_specs=(VMEM,) * 2,
         scratch_shapes=scatter_scratch(block, n_grp, n_dp, n_chip, jnp.float32, True) + [
-            pltpu.VMEM(g.shape, jnp.bfloat16),
-            pltpu.VMEM((n_grp - 2,) + g.shape, jnp.bfloat16),
+            dma((chunks,)), dma((chunks,)),
+        ],
+        compiler_params=params(collective),
+    )(x, features)
+
+
+def grads_kernel(n_grp, n_dp, chunks, *refs):
+    steps = grads_steps(n_grp, n_dp, chunks, *refs)
+    meet(next(steps))
+    for _ in steps:
+        pass
+
+
+def grads(x, n_grp, n_dp, chunks, collective):
+    dma = pltpu.SemaphoreType.DMA
+    side = max(n_dp - 1, 1)
+    return pl.pallas_call(
+        functools.partial(grads_kernel, n_grp, n_dp, chunks),
+        out_shape=jax.ShapeDtypeStruct((n_dp,) + x.shape, jnp.bfloat16),
+        in_specs=[VMEM],
+        out_specs=VMEM,
+        scratch_shapes=[
+            pltpu.VMEM(x.shape, jnp.bfloat16),
+            pltpu.VMEM((n_grp - 2,) + x.shape, jnp.bfloat16),
             dma((chunks,)), dma((chunks, n_grp - 2)),
             dma((chunks, 2)), dma((chunks,)),
             dma((chunks, side)), dma((chunks, side)),
-            dma((chunks,)), dma((chunks,)),
         ],
         compiler_params=params(collective),
-    )(x, features, g)
+    )(x)
 
 
 def local(tower_features, doc_weight, query_weight, positive_ids):
@@ -522,16 +538,18 @@
             total = term if total is None else total + term
         return total
 
-    dy = gather(back_norm(dpassage), n_grp, n_dp, n_chip, 1, False, 4).reshape(n_dp, rows, embed)
-    dquery, query_features, doc16 = back_sums(
-        dq_part.reshape(n_dp * n_mp, per_device, embed), features, weight_grad(swapped, dy),
-        n_grp, n_dp, n_chip, 8, 3,
+    dquery, query_features = back_sums(
+        dq_part.reshape(n_dp * n_mp, per_device, embed), features, n_grp, n_dp, n_chip, 8, 3
     )
     query_sides = [
         lax.ppermute(query_features, "dp", [(i, (i + s) % n_dp) for i in range(n_dp)]) if s else query_features
         for s in range(n_dp)
     ]
-    query_dy = gather(back_norm(dquery), n_grp, n_dp, n_chip, 4, True, 6).reshape(n_dp, rows, embed)
+    passage_dy, query_dy = lax.optimization_barrier((back_norm(dpassage), back_norm(dquery)))
+    dy = gather(passage_dy, n_grp, n_dp, n_chip, 1, False, 4).reshape(n_dp, rows, embed)
+    doc16 = grads(weight_grad(swapped, dy), n_grp, n_dp, 8, 5)
+    query_dy, query_sides, doc16 = lax.optimization_barrier((query_dy, query_sides, doc16))
+    query_dy = gather(query_dy, n_grp, n_dp, n_chip, 4, True, 6).reshape(n_dp, rows, embed)
     query_grad = weight_grad(query_sides, query_dy)
     rows_dy = lax.dynamic_index_in_dim(jnp.where(is_query, query_dy, dy), dp, 0, keepdims=False)
     back = lax.dot_general(

time: 277 us -> 237 us (0.86)
  waiting for transfers between devices: 14.9 us -> 0.01 us
  Pallas kernels: 215 us -> 201 us
  other arithmetic: 12 us -> 4.94 us
    pallas_call x1, Pallas kernels: 106 us -> 46.1 us  [back_sums(): pl.pallas_call(functools.partial(back_kernel, n_grp, n_dp, n_chip, chunks...]
    pallas_call x0 -> x1, Pallas kernels: none -> 46 us  [grads(): pl.pallas_call(functools.partial(grads_kernel, n_grp, n_dp, chunks), out_...]
    ppermute x1, waiting for transfers between devices: 14.9 us -> 0.01 us  [local(): lax.ppermute(query_features, 'dp', [(i, (i + s) % n_dp) for i in range(n_...]
    pallas_call x3, Pallas kernels: 80.7 us -> 84.1 us  [gather(): pl.pallas_call(functools.partial(gather_kernel, n_grp, n_dp, n_chip, chun...]
  transfers between devices with their start and end apart: 2 -> 2, of which waited for: 1 -> 0; matrix products, arithmetic and copies ran while one was open for 10% -> 6% of each run, Pallas kernels for 27% -> 73%
where the time goes in v4:
time: 237 us
  Pallas kernels  201 us (85%)
  matrix products  21.5 us (9%)
  other arithmetic  4.94 us (2%)
  starting transfers between devices  4.45 us (2%)
  between operations  2.66 us (1%)
    pallas_call x3, Pallas kernels, gather(): pl.pallas_call(functools.partial(gather_kernel, n_grp, n_dp, n_chip, chun...  84.1 us
    pallas_call x1, Pallas kernels, back_sums(): pl.pallas_call(functools.partial(back_kernel, n_grp, n_dp, n_chip, chunks...  46.1 us
    pallas_call x1, Pallas kernels, grads(): pl.pallas_call(functools.partial(grads_kernel, n_grp, n_dp, chunks), out_...  46 us
    pallas_call x1, Pallas kernels, scatter(): pl.pallas_call(functools.partial(scatter_kernel, n_grp, n_dp, n_chip), ou...  16.3 us
    dot_general x4, matrix products, weight_grad(): lax.dot_general(sides[s], lax.dynamic_index_in_dim(dy, lax.rem(dp + n_dp...  10.9 us
    pallas_call x1, Pallas kernels, stats(): pl.pallas_call(functools.partial(stats_kernel, n_grp, n_dp, n_mp), out_sh...  8.73 us
  transfers between devices with their start and end apart: 2, of which 0 were waited for; matrix products, arithmetic and copies ran while one was open for 6% of the time, Pallas kernels for 73%

profile of v4, /device:TPU:0, one launch (start us, length us, event | category | flops | bytes accessed | tf_op | source)
XLA Modules:
  0.0 236.7 jit_solution(5188050994229564827)
XLA Ops:
  0.6 1.9 dynamic-slice_bitcast_fusion
  2.5 3.0 %collective-permute-start.1 = (bf16[512,512]{1,0:T(8,128)(2,1)}, bf16[512,512]{1,0:T(8,128)(2,1)}, u32[]{:S(2)}, u32[]{:S(2)}) collective-permute-start(bf16[512,512]{1,0:T(8,128)(2,1)} %dynamic-slice_bitcast_fusion), channel_id=1, source_target_pairs={{0,4},{4,0},{1,5},{5,1},{2,6},{6,2},{3,7},{7,3},{8,12},{12,8},{9,1... | collective-permute-start | bytes 1572872 | tf_op jit(solution)/shard_map/ppermute | solution.py:492
  5.5 3.2 %fusion.15 = f32[1024,512]{0,1:T(8,128)S(1)} fusion(bf16[1024,1024]{1,0:T(8,128)(2,1)} %param.6, bf16[1024,1024]{1,0:T(8,128)(2,1)} %param.5, pred[]{:T(512)S(6)} %eq.16, bf16[1,512,1024]{2,1,0:T(8,128)(2,1)} %param.4), kind=kOutput, calls=%fused_computation.23 | convolution fusion | flops 1074790400 | bytes 7340033 | tf_op jit(solution)/shard_map/dot_general | solution.py:496
  8.7 16.3 %shard_map.75 = f32[128,1024]{1,0:T(8,128)S(1)} custom-call(f32[4,128,1024]{2,1,0:T(8,128)S(1)} %bitcast.58), custom_call_target="tpu_custom_call" | custom-call | tf_op jit(solution)/shard_map/pallas_call | solution.py:228
  25.0 0.1 multiply_reduce_fusion.2
  25.2 0.1 fusion.25.x_ref
  25.3 0.0 copy-start.4
  25.3 26.1 %shard_map.76 = bf16[8,128,1024]{2,1,0:T(8,128)(2,1)S(1)} custom-call(bf16[128,1024]{1,0:T(8,128)(2,1)S(1)} %fusion.25.x_ref), custom_call_target="tpu_custom_call" | custom-call | tf_op jit(solution)/shard_map/pallas_call | solution.py:121
  51.4 0.8 fusion.26
  52.3 0.0 copy-start.2
  52.3 0.2 exponential_reduce_fusion
  52.5 8.7 %shard_map.77 = f32[3,8,128]{2,1,0:T(8,128)S(1)} custom-call(f32[3,8,128]{2,1,0:T(8,128)S(1)} %pad_maximum_fusion.x_ref), custom_call_target="tpu_custom_call" | custom-call | tf_op jit(solution)/shard_map/pallas_call | solution.py:285
  61.3 0.6 fusion.23
  61.9 2.9 %convolution_multiply_fusion = f32[1024,1024]{1,0:T(8,128)} fusion(bf16[128,1024]{1,0:T(8,128)(2,1)S(1)} %fusion.25.x_ref, f32[1024,128]{0,1:T(8,128)S(1)} %get-tuple-element.29, f32[1024]{0:T(1024)S(1)} %get-tuple-element.26, s32[1024]{0:T(1024)S(1)} %copy-done.4, s32[128]{0:T(128)S(1)} %iota_add_fusion, pred[]{:T(512)S(6)} %not.3), kind=kOutput, calls=%fused_computation.1 | convolution fusion | flops 270663680 | bytes 4989441 | tf_op jit(solution)/shard_map/dot_general | solution.py:520
  64.8 46.1 %shard_map.78 = (f32[128,1024]{1,0:T(8,128)S(1)}, bf16[512,1024]{1,0:T(8,128)(2,1)}) custom-call(f32[8,128,1024]{2,1,0:T(8,128)} %bitcast.59, bf16[512,1024]{1,0:T(8,128)(2,1)S(1)} %bitcast.57), custom_call_target="tpu_custom_call" | custom-call | tf_op jit(solution)/shard_map/pallas_call | solution.py:435
  110.9 1.5 collective-permute-start
  112.3 0.0 copy-done.3
  112.3 1.4 multiply_reduce_fusion
  113.8 1.3 divide_convert_fusion
  115.0 0.0 copy-start.1
  115.0 30.4 %shard_map.79 = bf16[8,128,1024]{2,1,0:T(8,128)(2,1)S(1)} custom-call(bf16[128,1024]{1,0:T(8,128)(2,1)S(1)} %get-tuple-element.15.x_ref), custom_call_target="tpu_custom_call" | custom-call | tf_op jit(solution)/shard_map/pallas_call | solution.py:121
  146.2 0.7 fusion.8
  146.9 0.0 collective-permute-done.1
  146.9 3.1 %convolution_add_fusion.1.refs_0_ = f32[512,1024]{1,0:T(8,128)} fusion(f32[512,1024]{1,0:T(8,128)S(1)} %fusion.8, bf16[512,512]{1,0:T(8,128)(2,1)} %collective-permute-done.1, bf16[2,512,1024]{2,1,0:T(8,128)(2,1)S(1)} %bitcast.55, s32[]{:T(128)S(6)} %select_n.95), kind=kOutput, calls=%fused_computation.4 | convolution fusion | flops 537395200 | bytes 5767172 | tf_op jit(solution)/shard_map/dot_general | solution.py:532
  150.0 46.0 %shard_map.80 = bf16[2,512,1024]{2,1,0:T(8,128)(2,1)S(1)} custom-call(f32[512,1024]{1,0:T(8,128)} %convolution_add_fusion.1.refs_0_), custom_call_target="tpu_custom_call" | custom-call | tf_op jit(solution)/shard_map/pallas_call | solution.py:460
  196.0 0.0 copy-start.5
  196.0 0.0 collective-permute-done
  196.0 27.5 %shard_map.81 = bf16[8,128,1024]{2,1,0:T(8,128)(2,1)S(1)} custom-call(bf16[128,1024]{1,0:T(8,128)(2,1)S(1)} %get-tuple-element.18.x_ref), custom_call_target="tpu_custom_call" | custom-call | tf_op jit(solution)/shard_map/pallas_call | solution.py:121
  223.5 2.3 fusion
  225.8 2.5 %fusion.4 = f32[1024,1024]{1,0:T(8,128)S(1)} fusion(bf16[512,1024]{1,0:T(8,128)(2,1)} %collective-permute-done, bf16[2,512,1024]{2,1,0:T(8,128)(2,1)S(1)} %bitcast.50, s32[]{:T(128)S(6)} %select_n.95), kind=kOutput, calls=%fused_computation.12 | convolution fusion | flops 1073741824 | bytes 6291460 | tf_op jit(solution)/shard_map/dot_general | solution.py:532
  228.3 2.6 %bitcast_convert_fusion = f32[1024,1024]{1,0:T(8,128)} fusion(bf16[2,512,1024]{2,1,0:T(8,128)(2,1)S(1)} %shard_map.80), kind=kLoop, calls=%fused_computation.2 | loop fusion | flops 1048576 | bytes 6291456 | tf_op jit(solution)/shard_map/convert_element_type | solution.py:558
  230.9 4.6 %convolution_add_fusion = f32[1024,1024]{1,0:T(8,128)} fusion(f32[1024,1024]{1,0:T(8,128)S(1)} %fusion.4, bf16[512,1024]{1,0:T(8,128)(2,1)} %get-tuple-element.17, bf16[2,512,1024]{2,1,0:T(8,128)(2,1)S(1)} %bitcast.51, s32[]{:T(128)S(6)} %select_n.93), kind=kOutput, calls=%fused_computation | convolution fusion | flops 1074790400 | bytes 10485764 | tf_op jit(solution)/shard_map/dot_general | solution.py:532
  (13 shorter events, 0.0 us)
Async XLA Ops:
  2.5 144.4 %collective-permute-start.1 = (bf16[512,512]{1,0:T(8,128)(2,1)}, bf16[512,512]{1,0:T(8,128)(2,1)}, u32[]{:S(2)}, u32[]{:S(2)}) collective-permute-start(bf16[512,512]{1,0:T(8,128)(2,1)} %dynamic-slice_bitcast_fusion), channel_id=1, source_target_pairs={{0,4},{4,0},{1,5},{5,1},{2,6},{6,2},{3,7},{7,3},{8,12},{12,8},{9,1... | collective-permute-start | bytes 1572872 | tf_op jit(solution)/shard_map/ppermute | solution.py:492
  25.3 27.0 %copy-start.4 = (s32[1024]{0:T(1024)S(1)}, s32[1024]{0:T(1024)}, u32[]{:S(2)}) copy-start(s32[1024]{0:T(1024)} %param.7) | copy-start | bytes 12292
  52.3 12.5 %copy-start.2 = (f32[1024,128]{0,1:T(8,128)}, f32[1024,128]{0,1:T(8,128)S(1)}, u32[]{:S(2)}) copy-start(f32[1024,128]{0,1:T(8,128)S(1)} %get-tuple-element.29) | copy-start | bytes 1572868
  61.9 2.9 %copy-start = (bf16[1,512,1024]{2,1,0:T(8,128)(2,1)S(1)}, bf16[1,512,1024]{2,1,0:T(8,128)(2,1)}, u32[]{:S(2)}) copy-start(bf16[1,512,1024]{2,1,0:T(8,128)(2,1)} %param.4) | copy-start | bytes 3145732
  64.8 47.6 %copy-start.3 = (f32[1024,128]{0,1:T(8,128)S(1)}, f32[1024,128]{0,1:T(8,128)}, u32[]{:S(2)}) copy-start(f32[1024,128]{0,1:T(8,128)} %copy-done.2) | copy-start | bytes 1572868
  110.9 85.2 %collective-permute-start = (bf16[512,1024]{1,0:T(8,128)(2,1)}, bf16[512,1024]{1,0:T(8,128)(2,1)}, u32[]{:S(2)}, u32[]{:S(2)}) collective-permute-start(bf16[512,1024]{1,0:T(8,128)(2,1)} %get-tuple-element.17), channel_id=1, source_target_pairs={{0,4},{4,0},{1,5},{5,1},{2,6},{6,2},{3,7},{7,3},{8,12},{12,8},{9,1... | collective-permute-start | bytes 3145736 | tf_op jit(solution)/shard_map/ppermute | solution.py:545
  115.0 31.1 %copy-start.1 = (bf16[1,512,1024]{2,1,0:T(8,128)(2,1)S(1)}, bf16[1,512,1024]{2,1,0:T(8,128)(2,1)}, u32[]{:S(2)}) copy-start(bf16[1,512,1024]{2,1,0:T(8,128)(2,1)} %param.4) | copy-start | bytes 3145732
  150.0 73.5 %copy-start.6 = (bf16[1024,1024]{1,0:T(8,128)(2,1)S(1)}, bf16[1024,1024]{1,0:T(8,128)(2,1)}, u32[]{:S(2)}) copy-start(bf16[1024,1024]{1,0:T(8,128)(2,1)} %param.5) | copy-start | bytes 6291460
  196.0 27.5 %copy-start.5 = (bf16[1024,1024]{1,0:T(8,128)(2,1)S(1)}, bf16[1024,1024]{1,0:T(8,128)(2,1)}, u32[]{:S(2)}) copy-start(bf16[1024,1024]{1,0:T(8,128)(2,1)} %param.6) | copy-start | bytes 6291460

commit v5 on v4

--- a/solution.py
+++ b/solution.py
@@ -541,12 +541,13 @@
     dquery, query_features = back_sums(
         dq_part.reshape(n_dp * n_mp, per_device, embed), features, n_grp, n_dp, n_chip, 8, 3
     )
+    passage_dy, query_dy = lax.optimization_barrier((back_norm(dpassage), back_norm(dquery)))
+    dy = gather(passage_dy, n_grp, n_dp, n_chip, 1, False, 4).reshape(n_dp, rows, embed)
+    dy, query_features = lax.optimization_barrier((dy, query_features))
     query_sides = [
         lax.ppermute(query_features, "dp", [(i, (i + s) % n_dp) for i in range(n_dp)]) if s else query_features
         for s in range(n_dp)
     ]
-    passage_dy, query_dy = lax.optimization_barrier((back_norm(dpassage), back_norm(dquery)))
-    dy = gather(passage_dy, n_grp, n_dp, n_chip, 1, False, 4).reshape(n_dp, rows, embed)
     doc16 = grads(weight_grad(swapped, dy), n_grp, n_dp, 8, 5)
     query_dy, query_sides, doc16 = lax.optimization_barrier((query_dy, query_sides, doc16))
     query_dy = gather(query_dy, n_grp, n_dp, n_chip, 4, True, 6).reshape(n_dp, rows, embed)

time: 237 us -> 251 us (1.059)
  waiting for transfers between devices: 0.01 us -> 32.7 us
  Pallas kernels: 201 us -> 188 us
    ppermute x1, waiting for transfers between devices: 0.01 us -> 32.7 us  [local(): lax.ppermute(blocks[s], 'dp', [(i, (i + s) % n_dp) for i in range(n_dp)])]
    pallas_call x3, Pallas kernels: 84.1 us -> 68.9 us  [gather(): pl.pallas_call(functools.partial(gather_kernel, n_grp, n_dp, n_chip, chun...]
  transfers between devices with their start and end apart: 2 -> 2, of which waited for: 0 -> 1; matrix products, arithmetic and copies ran while one was open for 6% -> 2% of each run, Pallas kernels for 73% -> 18%
where the time goes in v5:
time: 251 us
  Pallas kernels  188 us (75%)
  waiting for transfers between devices  32.7 us (13%)
  matrix products  20.8 us (8%)
  other arithmetic  3.91 us (2%)
  between operations  2.62 us (1%)
    pallas_call x3, Pallas kernels, gather(): pl.pallas_call(functools.partial(gather_kernel, n_grp, n_dp, n_chip, chun...  68.9 us
    pallas_call x1, Pallas kernels, back_sums(): pl.pallas_call(functools.partial(back_kernel, n_grp, n_dp, n_chip, chunks...  46 us
    pallas_call x1, Pallas kernels, grads(): pl.pallas_call(functools.partial(grads_kernel, n_grp, n_dp, chunks), out_...  45.9 us
    ppermute x1, waiting for transfers between devices, local(): lax.ppermute(blocks[s], 'dp', [(i, (i + s) % n_dp) for i in range(n_dp)])  32.7 us
    pallas_call x1, Pallas kernels, scatter(): pl.pallas_call(functools.partial(scatter_kernel, n_grp, n_dp, n_chip), ou...  17.3 us
    dot_general x4, matrix products, weight_grad(): lax.dot_general(sides[s], lax.dynamic_index_in_dim(dy, lax.rem(dp + n_dp...  10.9 us
    pallas_call x1, Pallas kernels, stats(): pl.pallas_call(functools.partial(stats_kernel, n_grp, n_dp, n_mp), out_sh...  9.75 us
  transfers between devices with their start and end apart: 2, of which 1 were waited for; matrix products, arithmetic and copies ran while one was open for 2% of the time, Pallas kernels for 18%

profile of v5, /device:TPU:0, one launch (start us, length us, event | category | flops | bytes accessed | tf_op | source)
XLA Modules:
  0.0 250.8 jit_solution(16036941330061380057)
XLA Ops:
  0.6 3.2 %fusion.15 = f32[1024,512]{0,1:T(8,128)S(1)} fusion(bf16[1024,1024]{1,0:T(8,128)(2,1)} %param.6, bf16[1024,1024]{1,0:T(8,128)(2,1)} %param.5, pred[]{:T(512)S(6)} %eq.16, bf16[1,512,1024]{2,1,0:T(8,128)(2,1)} %param.4), kind=kOutput, calls=%fused_computation.23 | convolution fusion | flops 1074790400 | bytes 7340033 | tf_op jit(solution)/shard_map/dot_general | solution.py:496
  3.8 17.3 %shard_map.75 = f32[128,1024]{1,0:T(8,128)S(1)} custom-call(f32[4,128,1024]{2,1,0:T(8,128)S(1)} %bitcast.58), custom_call_target="tpu_custom_call" | custom-call | tf_op jit(solution)/shard_map/pallas_call | solution.py:228
  21.1 0.1 multiply_reduce_fusion.2
  21.2 0.1 fusion.25.x_ref
  21.4 0.0 copy-start.2
  21.4 26.7 %shard_map.76 = bf16[8,128,1024]{2,1,0:T(8,128)(2,1)S(1)} custom-call(bf16[128,1024]{1,0:T(8,128)(2,1)S(1)} %fusion.25.x_ref), custom_call_target="tpu_custom_call" | custom-call | tf_op jit(solution)/shard_map/pallas_call | solution.py:121
  48.1 0.8 fusion.26
  48.9 0.0 copy-done.2
  49.0 0.2 exponential_reduce_fusion
  49.2 9.7 %shard_map.77 = f32[3,8,128]{2,1,0:T(8,128)S(1)} custom-call(f32[3,8,128]{2,1,0:T(8,128)S(1)} %pad_maximum_fusion.x_ref), custom_call_target="tpu_custom_call" | custom-call | tf_op jit(solution)/shard_map/pallas_call | solution.py:285
  58.9 0.6 fusion.23
  59.6 2.9 %convolution_multiply_fusion = f32[1024,1024]{1,0:T(8,128)} fusion(bf16[128,1024]{1,0:T(8,128)(2,1)S(1)} %fusion.25.x_ref, f32[1024,128]{0,1:T(8,128)S(1)} %get-tuple-element.33, f32[1024]{0:T(1024)S(1)} %get-tuple-element.30, s32[1024]{0:T(1024)S(1)} %copy-done.2, s32[128]{0:T(128)S(1)} %iota_add_fusion, pred[]{:T(512)S(6)} %not.3), kind=kOutput, calls=%fused_computation.1 | convolution fusion | flops 270663680 | bytes 4989441 | tf_op jit(solution)/shard_map/dot_general | solution.py:520
  62.4 0.0 copy-done
  62.4 46.0 %shard_map.78 = (f32[128,1024]{1,0:T(8,128)S(1)}, bf16[512,1024]{1,0:T(8,128)(2,1)}) custom-call(f32[8,128,1024]{2,1,0:T(8,128)} %bitcast.59, bf16[512,1024]{1,0:T(8,128)(2,1)S(1)} %bitcast.57), custom_call_target="tpu_custom_call" | custom-call | tf_op jit(solution)/shard_map/pallas_call | solution.py:435
  108.5 0.7 multiply_reduce_fusion
  109.2 0.2 divide_convert_fusion
  109.4 0.0 copy-start.1
  109.4 14.9 %shard_map.79 = bf16[8,128,1024]{2,1,0:T(8,128)(2,1)S(1)} custom-call(bf16[128,1024]{1,0:T(8,128)(2,1)S(1)} %get-tuple-element.16.x_ref), custom_call_target="tpu_custom_call" | custom-call | tf_op jit(solution)/shard_map/pallas_call | solution.py:121
  124.3 1.6 collective-permute-start
  125.8 0.8 dynamic-slice_bitcast_fusion
  126.7 0.5 collective-permute-start.1
  127.9 0.7 fusion.8
  128.6 32.7 %collective-permute-done.1 = bf16[512,512]{1,0:T(8,128)(2,1)} collective-permute-done((bf16[512,512]{1,0:T(8,128)(2,1)}, bf16[512,512]{1,0:T(8,128)(2,1)}, u32[]{:S(2)}, u32[]{:S(2)}) %collective-permute-start.1) | collective-permute-done | bytes 524320 | tf_op jit(solution)/shard_map/ppermute | solution.py:492
  161.3 3.1 %convolution_add_fusion.1.refs_0_ = f32[512,1024]{1,0:T(8,128)} fusion(f32[512,1024]{1,0:T(8,128)S(1)} %fusion.8, bf16[512,512]{1,0:T(8,128)(2,1)} %collective-permute-done.1, bf16[2,512,1024]{2,1,0:T(8,128)(2,1)S(1)} %bitcast.53, s32[]{:T(128)S(6)} %select_n.95), kind=kOutput, calls=%fused_computation.4 | convolution fusion | flops 537395200 | bytes 5767172 | tf_op jit(solution)/shard_map/dot_general | solution.py:532
  164.4 45.9 %shard_map.80 = bf16[2,512,1024]{2,1,0:T(8,128)(2,1)S(1)} custom-call(f32[512,1024]{1,0:T(8,128)} %convolution_add_fusion.1.refs_0_), custom_call_target="tpu_custom_call" | custom-call | tf_op jit(solution)/shard_map/pallas_call | solution.py:460
  210.3 0.0 copy-start.3
  210.3 0.0 collective-permute-done
  210.3 27.3 %shard_map.81 = bf16[8,128,1024]{2,1,0:T(8,128)(2,1)S(1)} custom-call(bf16[128,1024]{1,0:T(8,128)(2,1)S(1)} %get-tuple-element.22.x_ref), custom_call_target="tpu_custom_call" | custom-call | tf_op jit(solution)/shard_map/pallas_call | solution.py:121
  237.7 2.3 fusion
  240.0 2.5 %fusion.4 = f32[1024,1024]{1,0:T(8,128)S(1)} fusion(bf16[512,1024]{1,0:T(8,128)(2,1)} %collective-permute-done, bf16[2,512,1024]{2,1,0:T(8,128)(2,1)S(1)} %bitcast.50, s32[]{:T(128)S(6)} %select_n.95), kind=kOutput, calls=%fused_computation.12 | convolution fusion | flops 1073741824 | bytes 6291460 | tf_op jit(solution)/shard_map/dot_general | solution.py:532
  242.5 2.6 %bitcast_convert_fusion = f32[1024,1024]{1,0:T(8,128)} fusion(bf16[2,512,1024]{2,1,0:T(8,128)(2,1)S(1)} %shard_map.80), kind=kLoop, calls=%fused_computation.2 | loop fusion | flops 1048576 | bytes 6291456 | tf_op jit(solution)/shard_map/convert_element_type | solution.py:559
  245.1 4.6 %convolution_add_fusion = f32[1024,1024]{1,0:T(8,128)} fusion(f32[1024,1024]{1,0:T(8,128)S(1)} %fusion.4, bf16[512,1024]{1,0:T(8,128)(2,1)} %get-tuple-element.21, bf16[2,512,1024]{2,1,0:T(8,128)(2,1)S(1)} %bitcast.51, s32[]{:T(128)S(6)} %select_n.93), kind=kOutput, calls=%fused_computation | convolution fusion | flops 1074790400 | bytes 10485764 | tf_op jit(solution)/shard_map/dot_general | solution.py:532
  (9 shorter events, 0.0 us)
Async XLA Ops:
  21.4 27.6 %copy-start.2 = (s32[1024]{0:T(1024)S(1)}, s32[1024]{0:T(1024)}, u32[]{:S(2)}) copy-start(s32[1024]{0:T(1024)} %param.7) | copy-start | bytes 12292
  59.6 2.9 %copy-start = (bf16[1,512,1024]{2,1,0:T(8,128)(2,1)S(1)}, bf16[1,512,1024]{2,1,0:T(8,128)(2,1)}, u32[]{:S(2)}) copy-start(bf16[1,512,1024]{2,1,0:T(8,128)(2,1)} %param.4) | copy-start | bytes 3145732
  109.4 16.4 %copy-start.1 = (bf16[1,512,1024]{2,1,0:T(8,128)(2,1)S(1)}, bf16[1,512,1024]{2,1,0:T(8,128)(2,1)}, u32[]{:S(2)}) copy-start(bf16[1,512,1024]{2,1,0:T(8,128)(2,1)} %param.4) | copy-start | bytes 3145732
  124.3 86.1 %collective-permute-start = (bf16[512,1024]{1,0:T(8,128)(2,1)}, bf16[512,1024]{1,0:T(8,128)(2,1)}, u32[]{:S(2)}, u32[]{:S(2)}) collective-permute-start(bf16[512,1024]{1,0:T(8,128)(2,1)} %get-tuple-element.21), channel_id=1, source_target_pairs={{0,4},{4,0},{1,5},{5,1},{2,6},{6,2},{3,7},{7,3},{8,12},{12,8},{9,1... | collective-permute-start | bytes 3145736 | tf_op jit(solution)/shard_map/ppermute | solution.py:548
  126.7 34.7 %collective-permute-start.1 = (bf16[512,512]{1,0:T(8,128)(2,1)}, bf16[512,512]{1,0:T(8,128)(2,1)}, u32[]{:S(2)}, u32[]{:S(2)}) collective-permute-start(bf16[512,512]{1,0:T(8,128)(2,1)} %dynamic-slice_bitcast_fusion), channel_id=1, source_target_pairs={{0,4},{4,0},{1,5},{5,1},{2,6},{6,2},{3,7},{7,3},{8,12},{12,8},{9,1... | collective-permute-start | bytes 1572872 | tf_op jit(solution)/shard_map/ppermute | solution.py:492
  164.4 73.3 %copy-start.4 = (bf16[1024,1024]{1,0:T(8,128)(2,1)S(1)}, bf16[1024,1024]{1,0:T(8,128)(2,1)}, u32[]{:S(2)}) copy-start(bf16[1024,1024]{1,0:T(8,128)(2,1)} %param.5) | copy-start | bytes 6291460
  210.3 27.4 %copy-start.3 = (bf16[1024,1024]{1,0:T(8,128)(2,1)S(1)}, bf16[1024,1024]{1,0:T(8,128)(2,1)}, u32[]{:S(2)}) copy-start(bf16[1024,1024]{1,0:T(8,128)(2,1)} %param.6) | copy-start | bytes 6291460

commit v6 on v4

--- a/solution.py
+++ b/solution.py
@@ -378,33 +378,41 @@
             doc_side(c, i).wait()
 
 
-def feature_steps(n_grp, chunks, f_ref, qf_ref, send, recv):
-    grp = lax.axis_index("grp")
+def feature_steps(n_grp, n_dp, chunks, f_ref, qf_ref, send, recv, ys, yr):
+    grp, dp = lax.axis_index("grp"), lax.axis_index("dp")
     last = grp == n_grp - 1
     rows = f_ref.shape[0] // chunks
     under = {"grp": lax.rem(grp + n_grp - 1, n_grp)}
-    yield [{"grp": lax.rem(grp + 1, n_grp)}, under]
-
-    def hop(c, source):
-        piece = pl.ds(c * rows, rows)
-        return remote(source.at[piece], qf_ref.at[piece], send.at[c], recv.at[c], under)
+    aside = [{"dp": lax.rem(dp + d, n_dp)} for d in range(1, n_dp)]
+    yield [{"grp": lax.rem(grp + 1, n_grp)}, under] + aside
+
+    def hop(c):
+        here = qf_ref.at[dp, pl.ds(c * rows, rows)]
+        return remote(here, here, send.at[c], recv.at[c], under)
+
+    def side(c, i):
+        here = qf_ref.at[dp, pl.ds(c * rows, rows)]
+        return remote(here, here, ys.at[c, i], yr.at[c, i], aside[i])
 
     @pl.when(last)
     def _():
+        qf_ref[dp] = f_ref[...]
         for c in range(chunks):
-            hop(c, f_ref).start()
-        qf_ref[...] = f_ref[...]
+            hop(c).start()
 
     yield None
     for c in range(chunks):
 
         @pl.when(jnp.logical_not(last))
         def _():
-            hop(c, qf_ref).wait_recv()
+            hop(c).wait_recv()
 
         @pl.when(jnp.logical_and(grp > 0, jnp.logical_not(last)))
         def _():
-            hop(c, qf_ref).start()
+            hop(c).start()
+
+        for i in range(n_dp - 1):
+            side(c, i).start()
 
         yield None
 
@@ -412,12 +420,15 @@
 
         @pl.when(grp > 0)
         def _():
-            hop(c, qf_ref).wait_send()
+            hop(c).wait_send()
+
+        for i in range(n_dp - 1):
+            side(c, i).wait()
 
 
 def back_kernel(n_grp, n_dp, n_chip, chunks, x_ref, f_ref, out_ref, qf_ref, *scratch):
     sums = scatter_steps(n_grp, n_dp, n_chip, True, 8, x_ref, out_ref, *scratch[:10])
-    ways = feature_steps(n_grp, chunks, f_ref, qf_ref, *scratch[10:])
+    ways = feature_steps(n_grp, n_dp, chunks, f_ref, qf_ref, *scratch[10:])
     meet(next(sums) + next(ways))
     next(sums)
     next(ways)
@@ -436,12 +447,13 @@
         functools.partial(back_kernel, n_grp, n_dp, n_chip, chunks),
         out_shape=(
             jax.ShapeDtypeStruct(block, jnp.float32),
-            jax.ShapeDtypeStruct(features.shape, features.dtype),
+            jax.ShapeDtypeStruct((n_dp,) + features.shape, features.dtype),
         ),
         in_specs=[VMEM] * 2,
         out_specs=(VMEM,) * 2,
         scratch_shapes=scatter_scratch(block, n_grp, n_dp, n_chip, jnp.float32, True) + [
             dma((chunks,)), dma((chunks,)),
+            dma((chunks, max(n_dp - 1, 1))), dma((chunks, max(n_dp - 1, 1))),
         ],
         compiler_params=params(collective),
     )(x, features)
@@ -541,16 +553,17 @@
     dquery, query_features = back_sums(
         dq_part.reshape(n_dp * n_mp, per_device, embed), features, n_grp, n_dp, n_chip, 8, 3
     )
-    query_sides = [
-        lax.ppermute(query_features, "dp", [(i, (i + s) % n_dp) for i in range(n_dp)]) if s else query_features
-        for s in range(n_dp)
-    ]
     passage_dy, query_dy = lax.optimization_barrier((back_norm(dpassage), back_norm(dquery)))
     dy = gather(passage_dy, n_grp, n_dp, n_chip, 1, False, 4).reshape(n_dp, rows, embed)
     doc16 = grads(weight_grad(swapped, dy), n_grp, n_dp, 8, 5)
-    query_dy, query_sides, doc16 = lax.optimization_barrier((query_dy, query_sides, doc16))
+    query_dy, doc16 = lax.optimization_barrier((query_dy, doc16))
     query_dy = gather(query_dy, n_grp, n_dp, n_chip, 4, True, 6).reshape(n_dp, rows, embed)
-    query_grad = weight_grad(query_sides, query_dy)
+    query_grad = lax.dot_general(
+        query_features.reshape(n_dp * rows, width),
+        query_dy.reshape(n_dp * rows, embed),
+        (((0,), (0,)), ((), ())),
+        preferred_element_type=jnp.float32,
+    )
     rows_dy = lax.dynamic_index_in_dim(jnp.where(is_query, query_dy, dy), dp, 0, keepdims=False)
     back = lax.dot_general(
         rows_dy, weight, (((1,), (1,)), ((), ())), preferred_element_type=jnp.float32

time: 237 us -> 219 us (0.924)
  Pallas kernels: 201 us -> 187 us
  matrix products: 21.5 us -> 18.1 us
    pallas_call x3, Pallas kernels: 84.1 us -> 70.8 us  [gather(): pl.pallas_call(functools.partial(gather_kernel, n_grp, n_dp, n_chip, chun...]
    pallas_call x1, Pallas kernels: 46 us -> 37.4 us  [grads(): pl.pallas_call(functools.partial(grads_kernel, n_grp, n_dp, chunks), out_...]
    pallas_call x1, Pallas kernels: 46.1 us -> 53.3 us  [back_sums(): pl.pallas_call(functools.partial(back_kernel, n_grp, n_dp, n_chip, chunks...]
    dot_general x4 -> x2, matrix products: 10.9 us -> 3.84 us  [weight_grad(): lax.dot_general(sides[s], lax.dynamic_index_in_dim(dy, lax.rem(dp + n_dp...]
    dot_general x0 -> x1, matrix products: none -> 4.4 us  [local(): lax.dot_general(query_features.reshape(n_dp * rows, width), query_dy.resh...]
  transfers between devices with their start and end apart: 2 -> 1, of which waited for: 0 -> 0; matrix products, arithmetic and copies ran while one was open for 6% -> 4% of each run, Pallas kernels for 73% -> 55%
where the time goes in v6:
time: 219 us; the launch traced here: 218 us
  Pallas kernels  187 us (85%)
  matrix products  18.1 us (8%)
  local copies, waits for them, and re-layouts  4.22 us (2%)
  other arithmetic  4.02 us (2%)
  starting transfers between devices  2.97 us (1%)
  between operations  2.62 us (1%)
    pallas_call x3, Pallas kernels, gather(): pl.pallas_call(functools.partial(gather_kernel, n_grp, n_dp, n_chip, chun...  70.8 us
    pallas_call x1, Pallas kernels, back_sums(): pl.pallas_call(functools.partial(back_kernel, n_grp, n_dp, n_chip, chunks...  53.3 us
    pallas_call x1, Pallas kernels, grads(): pl.pallas_call(functools.partial(grads_kernel, n_grp, n_dp, chunks), out_...  37.4 us
    pallas_call x1, Pallas kernels, scatter(): pl.pallas_call(functools.partial(scatter_kernel, n_grp, n_dp, n_chip), ou...  16.3 us
    pallas_call x1, Pallas kernels, stats(): pl.pallas_call(functools.partial(stats_kernel, n_grp, n_dp, n_mp), out_sh...  8.73 us
    dot_general x1, matrix products, local(): lax.dot_general(query_features.reshape(n_dp * rows, width), query_dy.resh...  4.4 us
  transfers between devices with their start and end apart: 1, of which 0 were waited for; matrix products, arithmetic and copies ran while one was open for 4% of the time, Pallas kernels for 55%

profile of v6, /device:TPU:0, one launch (start us, length us, event | category | flops | bytes accessed | tf_op | source)
XLA Modules:
  0.0 218.5 jit_solution(4782487546920202269)
XLA Ops:
  0.6 1.9 dynamic-slice_bitcast_fusion
  2.5 3.0 %collective-permute-start = (bf16[512,512]{1,0:T(8,128)(2,1)}, bf16[512,512]{1,0:T(8,128)(2,1)}, u32[]{:S(2)}, u32[]{:S(2)}) collective-permute-start(bf16[512,512]{1,0:T(8,128)(2,1)} %dynamic-slice_bitcast_fusion), channel_id=1, source_target_pairs={{0,4},{4,0},{1,5},{5,1},{2,6},{6,2},{3,7},{7,3},{8,12},{12,8},{9,1... | collective-permute-start | bytes 1572872 | tf_op jit(solution)/shard_map/ppermute | solution.py:504
  5.5 3.2 %fusion.10 = f32[1024,512]{0,1:T(8,128)S(1)} fusion(bf16[1024,1024]{1,0:T(8,128)(2,1)} %param.6, bf16[1024,1024]{1,0:T(8,128)(2,1)} %param.5, pred[]{:T(512)S(6)} %eq.16, bf16[1,512,1024]{2,1,0:T(8,128)(2,1)} %param.4), kind=kOutput, calls=%fused_computation.17 | convolution fusion | flops 1074790400 | bytes 7340033 | tf_op jit(solution)/shard_map/dot_general | solution.py:508
  8.7 16.3 %shard_map.75 = f32[128,1024]{1,0:T(8,128)S(1)} custom-call(f32[4,128,1024]{2,1,0:T(8,128)S(1)} %bitcast.51), custom_call_target="tpu_custom_call" | custom-call | tf_op jit(solution)/shard_map/pallas_call | solution.py:228
  25.0 0.1 multiply_reduce_fusion.2
  25.2 0.1 fusion.18.x_ref
  25.3 0.0 copy-start.3
  25.3 26.1 %shard_map.76 = bf16[8,128,1024]{2,1,0:T(8,128)(2,1)S(1)} custom-call(bf16[128,1024]{1,0:T(8,128)(2,1)S(1)} %fusion.18.x_ref), custom_call_target="tpu_custom_call" | custom-call | tf_op jit(solution)/shard_map/pallas_call | solution.py:121
  51.4 0.8 fusion.19
  52.3 0.0 copy-done.3
  52.3 0.2 exponential_reduce_fusion
  52.5 8.7 %shard_map.77 = f32[3,8,128]{2,1,0:T(8,128)S(1)} custom-call(f32[3,8,128]{2,1,0:T(8,128)S(1)} %pad_maximum_fusion.x_ref), custom_call_target="tpu_custom_call" | custom-call | tf_op jit(solution)/shard_map/pallas_call | solution.py:285
  61.3 0.6 fusion.16
  61.9 2.9 %convolution_multiply_fusion = f32[1024,1024]{1,0:T(8,128)} fusion(bf16[128,1024]{1,0:T(8,128)(2,1)S(1)} %fusion.18.x_ref, f32[1024,128]{0,1:T(8,128)S(1)} %get-tuple-element.25, f32[1024]{0:T(1024)S(1)} %get-tuple-element.22, s32[1024]{0:T(1024)S(1)} %copy-done.3, s32[128]{0:T(128)S(1)} %iota_add_fusion, pred[]{:T(512)S(6)} %not.3), kind=kOutput, calls=%fused_computation | convolution fusion | flops 270663680 | bytes 4989441 | tf_op jit(solution)/shard_map/dot_general | solution.py:532
  64.7 0.0 copy-done
  64.7 53.3 %shard_map.78 = (f32[128,1024]{1,0:T(8,128)S(1)}, bf16[2,512,1024]{2,1,0:T(8,128)(2,1)S(1)}) custom-call(f32[8,128,1024]{2,1,0:T(8,128)} %bitcast.55, bf16[512,1024]{1,0:T(8,128)(2,1)S(1)} %bitcast.50), custom_call_target="tpu_custom_call" | custom-call | tf_op jit(solution)/shard_map/pallas_call | solution.py:446
  118.0 0.0 copy-start.1
  118.0 1.3 copy-done.1
  119.4 0.7 multiply_reduce_fusion
  120.1 0.2 divide_convert_fusion
  120.3 16.2 %shard_map.79 = bf16[8,128,1024]{2,1,0:T(8,128)(2,1)S(1)} custom-call(bf16[128,1024]{1,0:T(8,128)(2,1)S(1)} %get-tuple-element.12.x_ref), custom_call_target="tpu_custom_call" | custom-call | tf_op jit(solution)/shard_map/pallas_call | solution.py:121
  137.2 0.7 fusion.5
  137.9 0.0 collective-permute-done
  138.0 3.1 %convolution_add_fusion.refs_0_ = f32[512,1024]{1,0:T(8,128)} fusion(f32[512,1024]{1,0:T(8,128)S(1)} %fusion.5, bf16[512,512]{1,0:T(8,128)(2,1)} %collective-permute-done, bf16[2,512,1024]{2,1,0:T(8,128)(2,1)S(1)} %bitcast.46, s32[]{:T(128)S(6)} %select_n.93), kind=kOutput, calls=%fused_computation.3 | convolution fusion | flops 537395200 | bytes 5767172 | tf_op jit(solution)/shard_map/dot_general | solution.py:544
  141.0 37.4 %shard_map.80 = bf16[2,512,1024]{2,1,0:T(8,128)(2,1)S(1)} custom-call(f32[512,1024]{1,0:T(8,128)} %convolution_add_fusion.refs_0_), custom_call_target="tpu_custom_call" | custom-call | tf_op jit(solution)/shard_map/pallas_call | solution.py:472
  178.4 28.5 %shard_map.81 = bf16[8,128,1024]{2,1,0:T(8,128)(2,1)S(1)} custom-call(bf16[128,1024]{1,0:T(8,128)(2,1)S(1)} %get-tuple-element.15.x_ref), custom_call_target="tpu_custom_call" | custom-call | tf_op jit(solution)/shard_map/pallas_call | solution.py:121
  207.0 0.0 copy-start.4
  207.0 0.0 copy-start.5
  207.0 2.7 %bitcast_convert_fusion = f32[1024,1024]{1,0:T(8,128)} fusion(bf16[2,512,1024]{2,1,0:T(8,128)(2,1)S(1)} %shard_map.80), kind=kLoop, calls=%fused_computation.1 | loop fusion | flops 1048576 | bytes 6291456 | tf_op jit(solution)/shard_map/convert_element_type | solution.py:571
  209.7 1.0 copy-done.5
  210.7 2.3 %fusion = bf16[1,512,1024]{2,1,0:T(8,128)(2,1)} fusion(bf16[2,512,1024]{2,1,0:T(8,128)(2,1)S(1)} %bitcast.47, s32[]{:T(128)S(6)} %select_n.96, bf16[2,512,1024]{2,1,0:T(8,128)(2,1)S(1)} %bitcast.52, pred[]{:T(512)S(6)} %eq.16, bf16[1024,1024]{1,0:T(8,128)(2,1)S(1)} %copy-done.4, bf16[1024,1024]{1,0:T(8,128)(2,1)S(1)} %copy-done.5), kind=kOutput, calls=%fused_computation.5 | convolution fusion | flops 1075838976 | bytes 7341568 | tf_op jit(solution)/shard_map/dot_general | solution.py:568
  213.0 4.4 %fusion.20 = f32[1024,1024]{1,0:T(8,128)} fusion(bf16[1024,1024]{1,0:T(8,128)(2,1)S(1)} %bitcast.54, bf16[1024,1024]{1,0:T(8,128)(2,1)S(1)} %bitcast.53), kind=kOutput, calls=%fused_computation.45 | convolution fusion | flops 2147483648 | bytes 8388608 | tf_op jit(solution)/shard_map/dot_general | solution.py:561
  (8 shorter events, 0.0 us)
Async XLA Ops:
  2.5 135.4 %collective-permute-start = (bf16[512,512]{1,0:T(8,128)(2,1)}, bf16[512,512]{1,0:T(8,128)(2,1)}, u32[]{:S(2)}, u32[]{:S(2)}) collective-permute-start(bf16[512,512]{1,0:T(8,128)(2,1)} %dynamic-slice_bitcast_fusion), channel_id=1, source_target_pairs={{0,4},{4,0},{1,5},{5,1},{2,6},{6,2},{3,7},{7,3},{8,12},{12,8},{9,1... | collective-permute-start | bytes 1572872 | tf_op jit(solution)/shard_map/ppermute | solution.py:504
  25.3 27.0 %copy-start.3 = (s32[1024]{0:T(1024)S(1)}, s32[1024]{0:T(1024)}, u32[]{:S(2)}) copy-start(s32[1024]{0:T(1024)} %param.7) | copy-start | bytes 12292
  61.9 2.9 %copy-start = (bf16[1,512,1024]{2,1,0:T(8,128)(2,1)S(1)}, bf16[1,512,1024]{2,1,0:T(8,128)(2,1)}, u32[]{:S(2)}) copy-start(bf16[1,512,1024]{2,1,0:T(8,128)(2,1)} %param.4) | copy-start | bytes 3145732
  118.0 1.4 copy-start.1
  207.0 2.8 %copy-start.4 = (bf16[1024,1024]{1,0:T(8,128)(2,1)S(1)}, bf16[1024,1024]{1,0:T(8,128)(2,1)}, u32[]{:S(2)}) copy-start(bf16[1024,1024]{1,0:T(8,128)(2,1)} %param.6) | copy-start | bytes 6291460
  207.0 3.7 %copy-start.5 = (bf16[1024,1024]{1,0:T(8,128)(2,1)S(1)}, bf16[1024,1024]{1,0:T(8,128)(2,1)}, u32[]{:S(2)}) copy-start(bf16[1024,1024]{1,0:T(8,128)(2,1)} %param.5) | copy-start | bytes 6291460
  210.7 2.3 %copy-start.2 = (bf16[2,512,1024]{2,1,0:T(8,128)(2,1)S(1)}, bf16[2,512,1024]{2,1,0:T(8,128)(2,1)}, u32[]{:S(2)}) copy-start(bf16[2,512,1024]{2,1,0:T(8,128)(2,1)} %copy-done.1) | copy-start | bytes 6291460

commit v7 on v6

--- a/solution.py
+++ b/solution.py
@@ -512,7 +512,7 @@
     row_norms = jnp.sqrt(jnp.sum(summed * summed, axis=-1, keepdims=True) + epsilon_norm)
     unit_rows = summed / row_norms
     embedded = unit_rows.astype(jnp.bfloat16)
-    queries_all = gather(embedded, n_grp, n_dp, n_chip, 4, True, 1).reshape(-1, embed)
+    queries_all = gather(embedded, n_grp, n_dp, n_chip, 8, True, 1).reshape(-1, embed)
     total_q = queries_all.shape[0]
     logits = inverse_temp * lax.dot_general(
         queries_all, embedded, (((1,), (1,)), ((), ())), preferred_element_type=jnp.float32
@@ -555,9 +555,9 @@
     )
     passage_dy, query_dy = lax.optimization_barrier((back_norm(dpassage), back_norm(dquery)))
     dy = gather(passage_dy, n_grp, n_dp, n_chip, 1, False, 4).reshape(n_dp, rows, embed)
-    doc16 = grads(weight_grad(swapped, dy), n_grp, n_dp, 8, 5)
+    doc16 = grads(weight_grad(swapped, dy), n_grp, n_dp, 16, 5)
     query_dy, doc16 = lax.optimization_barrier((query_dy, doc16))
-    query_dy = gather(query_dy, n_grp, n_dp, n_chip, 4, True, 6).reshape(n_dp, rows, embed)
+    query_dy = gather(query_dy, n_grp, n_dp, n_chip, 8, True, 6).reshape(n_dp, rows, embed)
     query_grad = lax.dot_general(
         query_features.reshape(n_dp * rows, width),
         query_dy.reshape(n_dp * rows, embed),

time: 219 us -> 214 us (0.977)
  Pallas kernels: 187 us -> 182 us
    pallas_call x3, Pallas kernels: 70.8 us -> 66.9 us  [gather(): pl.pallas_call(functools.partial(gather_kernel, n_grp, n_dp, n_chip, chun...]
  transfers between devices with their start and end apart: 1 -> 1, of which waited for: 0 -> 0; matrix products, arithmetic and copies ran while one was open for 4% -> 5% of each run, Pallas kernels for 55% -> 56%
where the time goes in v7:
time: 214 us
  Pallas kernels  182 us (85%)
  matrix products  18.1 us (8%)
  local copies, waits for them, and re-layouts  4.22 us (2%)
  other arithmetic  4.02 us (2%)
  starting transfers between devices  2.97 us (1%)
  between operations  2.62 us (1%)
    pallas_call x3, Pallas kernels, gather(): pl.pallas_call(functools.partial(gather_kernel, n_grp, n_dp, n_chip, chun...  66.9 us
    pallas_call x1, Pallas kernels, back_sums(): pl.pallas_call(functools.partial(back_kernel, n_grp, n_dp, n_chip, chunks...  53.3 us
    pallas_call x1, Pallas kernels, grads(): pl.pallas_call(functools.partial(grads_kernel, n_grp, n_dp, chunks), out_...  36.1 us
    pallas_call x1, Pallas kernels, scatter(): pl.pallas_call(functools.partial(scatter_kernel, n_grp, n_dp, n_chip), ou...  16.3 us
    pallas_call x1, Pallas kernels, stats(): pl.pallas_call(functools.partial(stats_kernel, n_grp, n_dp, n_mp), out_sh...  8.87 us
    dot_general x1, matrix products, local(): lax.dot_general(query_features.reshape(n_dp * rows, width), query_dy.resh...  4.4 us
  transfers between devices with their start and end apart: 1, of which 0 were waited for; matrix products, arithmetic and copies ran while one was open for 5% of the time, Pallas kernels for 56%

profile of v7, /device:TPU:0, one launch (start us, length us, event | category | flops | bytes accessed | tf_op | source)
XLA Modules:
  0.0 213.6 jit_solution(4233560739941153474)
XLA Ops:
  0.6 1.9 dynamic-slice_bitcast_fusion
  2.5 3.0 %collective-permute-start = (bf16[512,512]{1,0:T(8,128)(2,1)}, bf16[512,512]{1,0:T(8,128)(2,1)}, u32[]{:S(2)}, u32[]{:S(2)}) collective-permute-start(bf16[512,512]{1,0:T(8,128)(2,1)} %dynamic-slice_bitcast_fusion), channel_id=1, source_target_pairs={{0,4},{4,0},{1,5},{5,1},{2,6},{6,2},{3,7},{7,3},{8,12},{12,8},{9,1... | collective-permute-start | bytes 1572872 | tf_op jit(solution)/shard_map/ppermute | solution.py:504
  5.5 3.2 %fusion.10 = f32[1024,512]{0,1:T(8,128)S(1)} fusion(bf16[1024,1024]{1,0:T(8,128)(2,1)} %param.6, bf16[1024,1024]{1,0:T(8,128)(2,1)} %param.5, pred[]{:T(512)S(6)} %eq.16, bf16[1,512,1024]{2,1,0:T(8,128)(2,1)} %param.4), kind=kOutput, calls=%fused_computation.17 | convolution fusion | flops 1074790400 | bytes 7340033 | tf_op jit(solution)/shard_map/dot_general | solution.py:508
  8.7 16.3 %shard_map.75 = f32[128,1024]{1,0:T(8,128)S(1)} custom-call(f32[4,128,1024]{2,1,0:T(8,128)S(1)} %bitcast.51), custom_call_target="tpu_custom_call" | custom-call | tf_op jit(solution)/shard_map/pallas_call | solution.py:228
  25.0 0.1 multiply_reduce_fusion.2
  25.2 0.1 fusion.18.x_ref
  25.3 0.0 copy-start.3
  25.3 24.8 %shard_map.76 = bf16[8,128,1024]{2,1,0:T(8,128)(2,1)S(1)} custom-call(bf16[128,1024]{1,0:T(8,128)(2,1)S(1)} %fusion.18.x_ref), custom_call_target="tpu_custom_call" | custom-call | tf_op jit(solution)/shard_map/pallas_call | solution.py:121
  50.1 0.8 fusion.19
  51.0 0.0 copy-done.3
  51.0 0.2 exponential_reduce_fusion
  51.2 8.9 %shard_map.77 = f32[3,8,128]{2,1,0:T(8,128)S(1)} custom-call(f32[3,8,128]{2,1,0:T(8,128)S(1)} %pad_maximum_fusion.x_ref), custom_call_target="tpu_custom_call" | custom-call | tf_op jit(solution)/shard_map/pallas_call | solution.py:285
  60.1 0.6 fusion.16
  60.7 2.9 %convolution_multiply_fusion = f32[1024,1024]{1,0:T(8,128)} fusion(bf16[128,1024]{1,0:T(8,128)(2,1)S(1)} %fusion.18.x_ref, f32[1024,128]{0,1:T(8,128)S(1)} %get-tuple-element.25, f32[1024]{0:T(1024)S(1)} %get-tuple-element.22, s32[1024]{0:T(1024)S(1)} %copy-done.3, s32[128]{0:T(128)S(1)} %iota_add_fusion, pred[]{:T(512)S(6)} %not.3), kind=kOutput, calls=%fused_computation | convolution fusion | flops 270663680 | bytes 4989441 | tf_op jit(solution)/shard_map/dot_general | solution.py:532
  63.6 0.0 copy-done
  63.6 53.3 %shard_map.78 = (f32[128,1024]{1,0:T(8,128)S(1)}, bf16[2,512,1024]{2,1,0:T(8,128)(2,1)S(1)}) custom-call(f32[8,128,1024]{2,1,0:T(8,128)} %bitcast.55, bf16[512,1024]{1,0:T(8,128)(2,1)S(1)} %bitcast.50), custom_call_target="tpu_custom_call" | custom-call | tf_op jit(solution)/shard_map/pallas_call | solution.py:446
  116.9 0.0 copy-start.1
  116.9 1.3 copy-done.1
  118.3 0.7 multiply_reduce_fusion
  119.0 0.2 divide_convert_fusion
  119.2 16.2 %shard_map.79 = bf16[8,128,1024]{2,1,0:T(8,128)(2,1)S(1)} custom-call(bf16[128,1024]{1,0:T(8,128)(2,1)S(1)} %get-tuple-element.12.x_ref), custom_call_target="tpu_custom_call" | custom-call | tf_op jit(solution)/shard_map/pallas_call | solution.py:121
  136.1 0.7 fusion.5
  136.9 0.0 collective-permute-done
  136.9 3.1 %convolution_add_fusion.refs_0_ = f32[512,1024]{1,0:T(8,128)} fusion(f32[512,1024]{1,0:T(8,128)S(1)} %fusion.5, bf16[512,512]{1,0:T(8,128)(2,1)} %collective-permute-done, bf16[2,512,1024]{2,1,0:T(8,128)(2,1)S(1)} %bitcast.46, s32[]{:T(128)S(6)} %select_n.93), kind=kOutput, calls=%fused_computation.3 | convolution fusion | flops 537395200 | bytes 5767172 | tf_op jit(solution)/shard_map/dot_general | solution.py:544
  140.0 36.1 %shard_map.80 = bf16[2,512,1024]{2,1,0:T(8,128)(2,1)S(1)} custom-call(f32[512,1024]{1,0:T(8,128)} %convolution_add_fusion.refs_0_), custom_call_target="tpu_custom_call" | custom-call | tf_op jit(solution)/shard_map/pallas_call | solution.py:472
  176.1 25.9 %shard_map.81 = bf16[8,128,1024]{2,1,0:T(8,128)(2,1)S(1)} custom-call(bf16[128,1024]{1,0:T(8,128)(2,1)S(1)} %get-tuple-element.15.x_ref), custom_call_target="tpu_custom_call" | custom-call | tf_op jit(solution)/shard_map/pallas_call | solution.py:121
  202.0 0.0 copy-start.4
  202.0 0.0 copy-start.5
  202.0 2.7 %bitcast_convert_fusion = f32[1024,1024]{1,0:T(8,128)} fusion(bf16[2,512,1024]{2,1,0:T(8,128)(2,1)S(1)} %shard_map.80), kind=kLoop, calls=%fused_computation.1 | loop fusion | flops 1048576 | bytes 6291456 | tf_op jit(solution)/shard_map/convert_element_type | solution.py:571
  204.8 1.0 copy-done.5
  205.8 2.3 %fusion = bf16[1,512,1024]{2,1,0:T(8,128)(2,1)} fusion(bf16[2,512,1024]{2,1,0:T(8,128)(2,1)S(1)} %bitcast.47, s32[]{:T(128)S(6)} %select_n.96, bf16[2,512,1024]{2,1,0:T(8,128)(2,1)S(1)} %bitcast.52, pred[]{:T(512)S(6)} %eq.16, bf16[1024,1024]{1,0:T(8,128)(2,1)S(1)} %copy-done.4, bf16[1024,1024]{1,0:T(8,128)(2,1)S(1)} %copy-done.5), kind=kOutput, calls=%fused_computation.5 | convolution fusion | flops 1075838976 | bytes 7341568 | tf_op jit(solution)/shard_map/dot_general | solution.py:568
  208.0 4.4 %fusion.20 = f32[1024,1024]{1,0:T(8,128)} fusion(bf16[1024,1024]{1,0:T(8,128)(2,1)S(1)} %bitcast.54, bf16[1024,1024]{1,0:T(8,128)(2,1)S(1)} %bitcast.53), kind=kOutput, calls=%fused_computation.45 | convolution fusion | flops 2147483648 | bytes 8388608 | tf_op jit(solution)/shard_map/dot_general | solution.py:561
  (8 shorter events, 0.0 us)
Async XLA Ops:
  2.5 134.4 %collective-permute-start = (bf16[512,512]{1,0:T(8,128)(2,1)}, bf16[512,512]{1,0:T(8,128)(2,1)}, u32[]{:S(2)}, u32[]{:S(2)}) collective-permute-start(bf16[512,512]{1,0:T(8,128)(2,1)} %dynamic-slice_bitcast_fusion), channel_id=1, source_target_pairs={{0,4},{4,0},{1,5},{5,1},{2,6},{6,2},{3,7},{7,3},{8,12},{12,8},{9,1... | collective-permute-start | bytes 1572872 | tf_op jit(solution)/shard_map/ppermute | solution.py:504
  25.3 25.7 %copy-start.3 = (s32[1024]{0:T(1024)S(1)}, s32[1024]{0:T(1024)}, u32[]{:S(2)}) copy-start(s32[1024]{0:T(1024)} %param.7) | copy-start | bytes 12292
  60.7 2.9 %copy-start = (bf16[1,512,1024]{2,1,0:T(8,128)(2,1)S(1)}, bf16[1,512,1024]{2,1,0:T(8,128)(2,1)}, u32[]{:S(2)}) copy-start(bf16[1,512,1024]{2,1,0:T(8,128)(2,1)} %param.4) | copy-start | bytes 3145732
  116.9 1.4 copy-start.1
  202.0 2.8 %copy-start.4 = (bf16[1024,1024]{1,0:T(8,128)(2,1)S(1)}, bf16[1024,1024]{1,0:T(8,128)(2,1)}, u32[]{:S(2)}) copy-start(bf16[1024,1024]{1,0:T(8,128)(2,1)} %param.6) | copy-start | bytes 6291460
  202.0 3.7 %copy-start.5 = (bf16[1024,1024]{1,0:T(8,128)(2,1)S(1)}, bf16[1024,1024]{1,0:T(8,128)(2,1)}, u32[]{:S(2)}) copy-start(bf16[1024,1024]{1,0:T(8,128)(2,1)} %param.5) | copy-start | bytes 6291460
  205.8 2.3 %copy-start.2 = (bf16[2,512,1024]{2,1,0:T(8,128)(2,1)S(1)}, bf16[2,512,1024]{2,1,0:T(8,128)(2,1)}, u32[]{:S(2)}) copy-start(bf16[2,512,1024]{2,1,0:T(8,128)(2,1)} %copy-done.1) | copy-start | bytes 6291460
